TPU v7x, 512 devices: a whole 4x4x16 slice. The times are simulated.
512 devices in a mesh: dp: 16 (over z), tensor: 8 (over x, core), vocab: 4 (over y).
Axes of the slice: x: 4, y: 4, z: 16, core: 2. Of those that a mesh axis runs over, the one named last changes fastest.
Arguments:
- features: bfloat16 [1024, 49152], P('dp', ('tensor', 'vocab')), may hold values from -80 to 80
- fc_weight: bfloat16 [49152, 16384], P(('tensor', 'vocab'), 'dp'), may hold values from -1 to 1
- norm_gain: float32 [16384], P('dp'), may hold values from 0.1 to 1.9
- head_weight: bfloat16 [16384, 16384], P('dp', ('tensor', 'vocab')), may hold values from -4 to 4
- draft_map: int32 [16384], P(('tensor', 'vocab')), may hold values from 0 to 98298, as said below
- drafted: int32 [1024], P('dp'), may hold values from 0 to 114681, as said below
Outputs:
- logprob: float32 [1024, 16384], P('dp', ('tensor', 'vocab'))
- drafted_logp: float32 [1024], P('dp')
Inputs may be any that keep to these rules, and one draw needn't show every extreme that they name: Draft id j stands for target id j + draft_map[j]; these target ids start at 0, rise strictly with j and stay below 128256. Every row's drafted id is the target id of exactly one draft id.
All inputs are finite; a program needn't handle non-finite values.
Results may differ from a plain program's by a relative error of at most 0.0029.
Values may be sent and summed in bfloat16 or wider, within the bound.
No kernel may reach another device: no remote copies, remote signals or barrier semaphores. Data moves between devices by JAX's collectives and lax.ppermute only.
A program may use at most 64 MiB of HBM per device.

v0:
```python
import jax
import jax.numpy as jnp
from jax import lax
from jax.sharding import PartitionSpec as P

eps = 1e-05
PLANE = ("tensor", "vocab")
f16, bf16, f32 = jnp.float16, jnp.bfloat16, jnp.float32

UP = 2.0**9
PARTIAL = 2.0**-2
SCALED = 2.0**-7
LEVEL = 2.0**-7
FINE = 2.0**11

Z = 16
PEERS = 16
CORE_PAIRS = [(i, i ^ 1) for i in range(8)]
SAME_CORE = [[(2 * x + c) * 4 + y for x in range(4) for y in range(4)] for c in range(2)]
SAME_PARITY = [[2 * i + p for i in range(Z // 2)] for p in range(2)]


def swap_cores(a):
    return lax.ppermute(a, "tensor", CORE_PAIRS)


def by_core(core, mine, other):
    return jnp.where(
        core == 0, jnp.concatenate([mine, other]), jnp.concatenate([other, mine])
    )


def exchange(a):
    return lax.all_to_all(a, PLANE, 0, 0, axis_index_groups=SAME_CORE)


def pick(a, i):
    return lax.dynamic_index_in_dim(a, i, 1, keepdims=False)


def levels(square, width):
    root = jnp.sqrt(square) * LEVEL
    high = root.astype(f16)
    low = ((root - high.astype(f32)) * FINE).astype(f16)
    pair = jnp.stack([high, low], axis=-2)
    pad = [(0, 0)] * (pair.ndim - 2) + [(0, 6), (0, width - pair.shape[-1])]
    return jnp.pad(pair, pad)


def squares(a, rows):
    high, low = a[..., -8, :rows].astype(f32), a[..., -7, :rows].astype(f32)
    return ((high + low * (1.0 / FINE)) * (1.0 / LEVEL)) ** 2


def body(features, fc_weight, norm_gain, head_weight, draft_map, drafted):
    core = lax.axis_index("tensor") % 2
    parity = lax.axis_index("dp") % 2
    depth = fc_weight.shape[1]
    width = head_weight.shape[1]
    rows = features.shape[0]
    half = rows // 2

    sent = (features.astype(f32) * UP).astype(f16).reshape(2, half, -1)
    every = lax.all_gather(sent, "dp", axis=1)

    def joined_part(h):
        block = lax.dynamic_index_in_dim(every, h, 0, keepdims=False).astype(bf16)
        return jnp.dot(block, fc_weight, preferred_element_type=f32) * (PARTIAL / UP)

    away = joined_part(1 - core).astype(f16)
    kept = lax.optimization_barrier((joined_part(core), away))[0]
    chip = (kept + swap_cores(away).astype(f32)).astype(f16)
    later = lax.optimization_barrier((head_weight, draft_map, chip))
    head_other, map_other = swap_cores(later[0]), swap_cores(later[1])
    joined = jnp.sum(exchange(chip).astype(f32), axis=0)
    scaled = (joined * (norm_gain * (SCALED / PARTIAL))).astype(f16)
    scaled = exchange(jnp.broadcast_to(scaled, (PEERS,) + scaled.shape))

    gain = lax.optimization_barrier((norm_gain, map_other))[0]
    own = scaled.astype(f32) * (1.0 / (gain * SCALED))
    square = (jnp.mean(own * own, axis=2) + eps).reshape(Z // 2, 2, half)
    scaled = scaled.reshape(Z // 2, 2, half, depth)

    def partial(h, weight):
        block = pick(scaled, h).astype(bf16).reshape(-1, depth)
        return jnp.dot(block, weight, preferred_element_type=f32)

    far_square = pick(square, 1 - parity).reshape(-1)
    near_square = pick(square, parity).reshape(-1)
    far_level = levels(far_square, width)
    count = far_square.shape[0]

    def through(weight, by):
        values = partial(1 - parity, weight) * (lax.rsqrt(far_square) * (1.0 / SCALED))[:, None]
        values = jnp.concatenate([values.astype(f16), far_level])
        return lax.ppermute(values, "dp", [(i, (i + by) % Z) for i in range(Z)])

    arrived = through(head_weight, 1), through(head_other, -1)
    sums, sum_squares = [], []
    for weight, got in zip((head_weight, head_other), arrived):
        got_square = squares(got, count)
        both = near_square + got_square
        here, there = lax.rsqrt(both) * (1.0 / SCALED), jnp.sqrt(got_square / both)
        got = partial(parity, weight) * here[:, None] + got[:count].astype(f32) * there[:, None]
        sums.append(got.astype(f16).reshape(-1, half, width))
        sum_squares.append(both.reshape(-1, half))
    packed = sums + [levels(jnp.concatenate(sum_squares, axis=1), width)]
    packed = jnp.concatenate(packed, axis=1)
    got = lax.all_to_all(packed, "dp", 0, 0, axis_index_groups=SAME_PARITY)
    square = squares(got, rows)
    back = jnp.sqrt(square / (jnp.sum(square, axis=0) / Z))
    logits = jnp.sum(got[:, :rows].astype(f32) * back[:, :, None], axis=0)

    logits = logits.reshape(2, half, width)
    here = 2 * lax.axis_index("tensor") + 2 * jnp.array([0, 1]) * (1 - 2 * core)
    here = (here * 2 + lax.axis_index("vocab")) * width
    target = jnp.stack([draft_map, map_other]) + jnp.arange(width, dtype=jnp.int32) + here[:, None]
    wanted = lax.dynamic_slice_in_dim(drafted, core * half, half)
    hit = wanted[None, :, None] == target[:, None, :]
    own_pick = jnp.sum(jnp.where(hit, logits, f32(0.0)), axis=(0, 2))
    own_top = jnp.max(logits, axis=(0, 2))
    own_total = jnp.sum(jnp.exp(logits - own_top[None, :, None]), axis=(0, 2))
    own = jnp.pad(jnp.stack([own_top, own_total, own_pick]), ((0, 5), (0, 128 - half)))
    every = exchange(jnp.broadcast_to(own, (PEERS,) + own.shape))[:, :, :half]
    top = jnp.max(every[:, 0], axis=0)
    total = jnp.sum(every[:, 1] * jnp.exp(every[:, 0] - top), axis=0)
    picked = jnp.sum(every[:, 2], axis=0)
    lse = top + jnp.log(total)
    logprob = logits - lse[None, :, None]
    picked = picked - lse
    away = jnp.concatenate([logprob[1], jnp.pad(picked[None], ((0, 7), (0, width - half)))])
    got = swap_cores(away)
    return (
        by_core(core, logprob[0], got[:half]),
        by_core(core, picked, got[half, :half]),
    )


def solution(mesh):
    placed = (
        P("dp", ("tensor", "vocab")),
        P(("tensor", "vocab"), "dp"),
        P("dp"),
        P("dp", ("tensor", "vocab")),
        P(("tensor", "vocab")),
        P("dp"),
    )
    return jax.shard_map(
        body,
        mesh=mesh,
        in_specs=placed,
        out_specs=(P("dp", ("tensor", "vocab")), P("dp")),
        check_vma=False,
    )
```

profile of v0, /device:TPU:65, one launch (start us, length us, event | category | flops | bytes accessed | tf_op | source)
XLA Modules:
  0.0 206.7 jit_solution(7008789795293920511)
XLA Ops:
  0.7 1.1 multiply_convert_fusion.1
  1.8 50.9 %all-gather.1 = f16[2,16,32,1536]{3,2,1,0:T(8,128)(2,1)} all-gather(f16[2,1,32,1536]{3,2,1,0:T(8,128)(2,1)S(1)} %bitcast.56), channel_id=1, replica_groups=mesh['dp'=16,'tensor'=8,'vocab'=4] {'dp'}, dimensions={1}, use_global_device_ids=true | all-gather | bytes 3342336 | tf_op jit(solution)/shard_map/all_gather | solution.py:64
  52.7 4.2 %multiply_convert_fusion = f16[16,32,1024]{2,1,0:T(8,128)(2,1)} fusion(bf16[1536,1024]{1,0:T(8,128)(2,1)S(1)} %copy-done, f16[2,16,32,1536]{3,2,1,0:T(8,128)(2,1)} %all-gather.1, s32[]{:T(128)S(6)} %select_n.60), kind=kOutput, calls=%fused_computation.7 | convolution fusion | flops 1612447744 | bytes 5767172 | tf_op jit(solution)/shard_map/dot_general | solution.py:68
  56.9 10.6 %collective-permute-start = (f16[16,32,1024]{2,1,0:T(8,128)(2,1)}, f16[16,32,1024]{2,1,0:T(8,128)(2,1)}, u32[]{:S(2)}, u32[]{:S(2)}) collective-permute-start(f16[16,32,1024]{2,1,0:T(8,128)(2,1)} %multiply_convert_fusion), channel_id=1, source_target_pairs={{0,4},{4,0},{8,12},{12,8},{16,20},{20,16},{24,28},{28,24},{1,5},{5... | collective-permute-start | bytes 3145736 | tf_op jit(solution)/shard_map/ppermute | solution.py:24
  67.5 3.2 %fusion.4 = f32[16,32,1024]{2,1,0:T(8,128)S(1)} fusion(bf16[1536,1024]{1,0:T(8,128)(2,1)S(1)} %copy-done, f16[2,16,32,1536]{3,2,1,0:T(8,128)(2,1)} %all-gather.1, s32[]{:T(128)S(6)} %select_n.59), kind=kOutput, calls=%fused_computation.8 | convolution fusion | flops 1611923456 | bytes 6815748 | tf_op jit(solution)/shard_map/dot_general | solution.py:68
  70.8 2.6 %add_convert_fusion = f16[16,32,1024]{2,1,0:T(8,128)(2,1)} fusion(f32[16,32,1024]{2,1,0:T(8,128)S(1)} %fusion.4, f16[16,32,1024]{2,1,0:T(8,128)(2,1)} %collective-permute-done), kind=kLoop, calls=%fused_computation.6 | loop fusion | flops 1572864 | bytes 4194304 | tf_op jit(solution)/shard_map/convert_element_type | solution.py:72
  73.4 6.9 %all-to-all-start = ((f16[16,32,1024]{2,1,0:T(8,128)(2,1)}), f16[16,32,1024]{2,1,0:T(8,128)(2,1)}, u32[]{:S(2)}, u32[]{:S(2)}) async-start(f16[16,32,1024]{2,1,0:T(8,128)(2,1)} %add_convert_fusion), calls=%async_computation | async-start | bytes 2097152 | tf_op jit(solution)/shard_map/all_to_all | solution.py:34
  80.4 17.0 %all-to-all-done = f16[16,32,1024]{2,1,0:T(8,128)(2,1)} async-done(((f16[16,32,1024]{2,1,0:T(8,128)(2,1)}), f16[16,32,1024]{2,1,0:T(8,128)(2,1)}, u32[]{:S(2)}, u32[]{:S(2)}) %all-to-all-start) | async-done | bytes 1048608 | tf_op jit(solution)/shard_map/all_to_all | solution.py:34
  97.4 1.4 convert_reduce_fusion
  98.8 1.1 broadcast_in_dim.7
  100.0 4.3 %all-to-all-start.1 = ((f16[16,32,1024]{2,1,0:T(8,128)(2,1)}), f16[16,32,1024]{2,1,0:T(8,128)(2,1)}, u32[]{:S(2)}, u32[]{:S(2)}) async-start(f16[16,32,1024]{2,1,0:T(8,128)(2,1)} %broadcast_in_dim.7), calls=%async_computation.1 | async-start | bytes 2097152 | tf_op jit(solution)/shard_map/all_to_all | solution.py:34
  104.3 3.7 %collective-permute-start.1 = (s32[512]{0:T(512)S(1)}, s32[512]{0:T(512)S(1)}, u32[]{:S(2)}, u32[]{:S(2)}) collective-permute-start(s32[512]{0:T(512)S(1)} %copy-done.3), channel_id=1, source_target_pairs={{0,4},{4,0},{8,12},{12,8},{16,20},{20,16},{24,28},{28,24},{1,5},{5... | collective-permute-start | bytes 6152 | tf_op jit(solution)/shard_map/ppermute | solution.py:24
  108.0 1.9 collective-permute-start.3
  110.0 9.4 %all-to-all-done.1 = f16[16,32,1024]{2,1,0:T(8,128)(2,1)} async-done(((f16[16,32,1024]{2,1,0:T(8,128)(2,1)}), f16[16,32,1024]{2,1,0:T(8,128)(2,1)}, u32[]{:S(2)}, u32[]{:S(2)}) %all-to-all-start.1) | async-done | bytes 1048608 | tf_op jit(solution)/shard_map/all_to_all | solution.py:34
  119.4 1.6 multiply_reduce_fusion
  121.2 2.4 %dynamic-slice_convert_fusion.1 = (bf16[8,1,32,1024]{3,2,1,0:T(8,128)(2,1)}, bf16[8,1,32,1024]{3,2,1,0:T(8,128)(2,1)S(1)}) fusion(f16[8,2,32,1024]{3,2,1,0:T(8,128)(2,1)} %bitcast.4, s32[]{:T(128)S(6)} %select_n.62, s32[]{:T(128)S(6)} %select_n.63), kind=kLoop, calls=%fused_computation.29 | loop fusion | flops 524288 | bytes 2097160 | tf_op jit(solution)/shard_map/convert_element_type | solution.py:85
  124.1 1.7 fusion.17
  125.7 0.9 pad_maximum_fusion.1
  126.6 1.9 collective-permute-start.2
  128.5 3.4 %collective-permute-start.4 = (f16[264,512]{1,0:T(8,128)(2,1)S(1)}, f16[264,512]{1,0:T(8,128)(2,1)}, u32[]{:S(2)}, u32[]{:S(2)}) collective-permute-start(f16[264,512]{1,0:T(8,128)(2,1)S(1)} %get-tuple-element.30), channel_id=1, source_target_pairs={{0,480},{32,0},{64,32},{96,64},{128,96},{160,128},{192,160},{224,1... | collective-permute-start | bytes 811016 | tf_op jit(solution)/shard_map/ppermute | solution.py:96
  131.9 2.1 %collective-permute-done.2 = f16[264,512]{1,0:T(8,128)(2,1)} collective-permute-done((f16[264,512]{1,0:T(8,128)(2,1)}, f16[264,512]{1,0:T(8,128)(2,1)}, u32[]{:S(2)}, u32[]{:S(2)}) %collective-permute-start.2) | collective-permute-done | bytes 270368 | tf_op jit(solution)/shard_map/ppermute | solution.py:96
  134.1 2.0 collective-permute-done.4
  136.6 1.4 fusion.40
  138.3 1.9 add_convert_fusion.1
  140.3 1.7 fusion.18
  142.0 0.9 fusion.20
  142.9 9.4 %all-to-all-start.2 = ((f16[8,72,512]{2,1,0:T(8,128)(2,1)}), f16[8,72,512]{2,1,0:T(8,128)(2,1)}, u32[]{:S(2)}, u32[]{:S(2)}) async-start(f16[8,72,512]{2,1,0:T(8,128)(2,1)} %fusion.20), calls=%async_computation.2 | async-start | bytes 1179648 | tf_op jit(solution)/shard_map/all_to_all | solution.py:109
  152.5 28.7 %all-to-all-done.2 = f16[8,72,512]{2,1,0:T(8,128)(2,1)} async-done(((f16[8,72,512]{2,1,0:T(8,128)(2,1)}), f16[8,72,512]{2,1,0:T(8,128)(2,1)}, u32[]{:S(2)}, u32[]{:S(2)}) %all-to-all-start.2) | async-done | bytes 589856 | tf_op jit(solution)/shard_map/all_to_all | solution.py:109
  182.0 1.3 multiply_reduce_fusion.1
  184.1 10.0 %all_to_all.20 = f32[16,8,128]{2,1,0:T(8,128)S(1)} all-to-all(f32[16,8,128]{2,1,0:T(8,128)S(1)} %broadcast_in_dim.9), channel_id=1, replica_groups={{0,1,2,3,8,9,10,11,16,17,18,19,24,25,26,27},{4,5,6,7,12,13,14,15,20,21,..., dimensions={0} | all-to-all | bytes 131072 | tf_op jit(solution)/shard_map/all_to_all | solution.py:34
  194.3 10.2 %collective-permute-start.5 = (f32[40,512]{1,0:T(8,128)S(1)}, f32[40,512]{1,0:T(8,128)S(1)}, u32[]{:S(2)}, u32[]{:S(2)}) collective-permute-start(f32[40,512]{1,0:T(8,128)S(1)} %select_maximum_fusion), channel_id=1, source_target_pairs={{0,4},{4,0},{8,12},{12,8},{16,20},{20,16},{24,28},{28,24},{1,5},{5... | collective-permute-start | bytes 245768 | tf_op jit(solution)/shard_map/ppermute | solution.py:24
  204.5 0.9 collective-permute-done.5
  (63 shorter events, 4.9 us)
Async XLA Ops:
  0.6 52.1 %copy-start = (bf16[1536,1024]{1,0:T(8,128)(2,1)S(1)}, bf16[1536,1024]{1,0:T(8,128)(2,1)}, u32[]{:S(2)}) copy-start(bf16[1536,1024]{1,0:T(8,128)(2,1)} %param.8) | copy-start | bytes 9437188
  56.9 13.9 %collective-permute-start = (f16[16,32,1024]{2,1,0:T(8,128)(2,1)}, f16[16,32,1024]{2,1,0:T(8,128)(2,1)}, u32[]{:S(2)}, u32[]{:S(2)}) collective-permute-start(f16[16,32,1024]{2,1,0:T(8,128)(2,1)} %multiply_convert_fusion), channel_id=1, source_target_pairs={{0,4},{4,0},{8,12},{12,8},{16,20},{20,16},{24,28},{28,24},{1,5},{5... | collective-permute-start | bytes 3145736 | tf_op jit(solution)/shard_map/ppermute | solution.py:24
  73.4 7.0 %copy-start.2 = (f32[1024]{0:T(1024)S(1)}, f32[1024]{0:T(1024)}, u32[]{:S(2)}) copy-start(f32[1024]{0:T(1024)} %param.9) | copy-start | bytes 12292
  73.4 24.0 %all-to-all-start = ((f16[16,32,1024]{2,1,0:T(8,128)(2,1)}), f16[16,32,1024]{2,1,0:T(8,128)(2,1)}, u32[]{:S(2)}, u32[]{:S(2)}) async-start(f16[16,32,1024]{2,1,0:T(8,128)(2,1)} %add_convert_fusion), calls=%async_computation | async-start | bytes 2097152 | tf_op jit(solution)/shard_map/all_to_all | solution.py:34
  80.4 24.0 %copy-start.3 = (s32[512]{0:T(512)S(1)}, s32[512]{0:T(512)}, u32[]{:S(2)}) copy-start(s32[512]{0:T(512)} %param.11) | copy-start | bytes 6148
  100.0 19.5 %all-to-all-start.1 = ((f16[16,32,1024]{2,1,0:T(8,128)(2,1)}), f16[16,32,1024]{2,1,0:T(8,128)(2,1)}, u32[]{:S(2)}, u32[]{:S(2)}) async-start(f16[16,32,1024]{2,1,0:T(8,128)(2,1)} %broadcast_in_dim.7), calls=%async_computation.1 | async-start | bytes 2097152 | tf_op jit(solution)/shard_map/all_to_all | solution.py:34
  104.3 5.6 %collective-permute-start.1 = (s32[512]{0:T(512)S(1)}, s32[512]{0:T(512)S(1)}, u32[]{:S(2)}, u32[]{:S(2)}) collective-permute-start(s32[512]{0:T(512)S(1)} %copy-done.3), channel_id=1, source_target_pairs={{0,4},{4,0},{8,12},{12,8},{16,20},{20,16},{24,28},{28,24},{1,5},{5... | collective-permute-start | bytes 6152 | tf_op jit(solution)/shard_map/ppermute | solution.py:24
  108.0 16.0 %collective-permute-start.3 = (bf16[1024,512]{1,0:T(8,128)(2,1)}, bf16[1024,512]{1,0:T(8,128)(2,1)}, u32[]{:S(2)}, u32[]{:S(2)}) collective-permute-start(bf16[1024,512]{1,0:T(8,128)(2,1)} %param.10), channel_id=1, source_target_pairs={{0,4},{4,0},{8,12},{12,8},{16,20},{20,16},{24,28},{28,24},{1,5},{5... | collective-permute-start | bytes 3145736 | tf_op jit(solution)/shard_map/ppermute | solution.py:24
  121.2 2.4 %copy-start.4 = (bf16[1024,512]{1,0:T(8,128)(2,1)S(1)}, bf16[1024,512]{1,0:T(8,128)(2,1)}, u32[]{:S(2)}) copy-start(bf16[1024,512]{1,0:T(8,128)(2,1)} %param.10) | copy-start | bytes 3145732
  126.6 7.5 %collective-permute-start.2 = (f16[264,512]{1,0:T(8,128)(2,1)}, f16[264,512]{1,0:T(8,128)(2,1)}, u32[]{:S(2)}, u32[]{:S(2)}) collective-permute-start(f16[264,512]{1,0:T(8,128)(2,1)} %get-tuple-element.29), channel_id=1, source_target_pairs={{0,32},{32,64},{64,96},{96,128},{128,160},{160,192},{192,224},{224... | collective-permute-start | bytes 811016 | tf_op jit(solution)/shard_map/ppermute | solution.py:96
  128.5 7.6 %collective-permute-start.4 = (f16[264,512]{1,0:T(8,128)(2,1)S(1)}, f16[264,512]{1,0:T(8,128)(2,1)}, u32[]{:S(2)}, u32[]{:S(2)}) collective-permute-start(f16[264,512]{1,0:T(8,128)(2,1)S(1)} %get-tuple-element.30), channel_id=1, source_target_pairs={{0,480},{32,0},{64,32},{96,64},{128,96},{160,128},{192,160},{224,1... | collective-permute-start | bytes 811016 | tf_op jit(solution)/shard_map/ppermute | solution.py:96
  138.2 2.1 copy-start.1
  140.3 12.1 %copy-start.5 = (s32[64]{0:T(128)S(1)}, s32[64]{0:T(128)}, u32[]{:S(2)}) copy-start(s32[64]{0:T(128)} %param.12) | copy-start | bytes 772
  142.9 38.2 %all-to-all-start.2 = ((f16[8,72,512]{2,1,0:T(8,128)(2,1)}), f16[8,72,512]{2,1,0:T(8,128)(2,1)}, u32[]{:S(2)}, u32[]{:S(2)}) async-start(f16[8,72,512]{2,1,0:T(8,128)(2,1)} %fusion.20), calls=%async_computation.2 | async-start | bytes 1179648 | tf_op jit(solution)/shard_map/all_to_all | solution.py:109
  194.3 11.1 %collective-permute-start.5 = (f32[40,512]{1,0:T(8,128)S(1)}, f32[40,512]{1,0:T(8,128)S(1)}, u32[]{:S(2)}, u32[]{:S(2)}) collective-permute-start(f32[40,512]{1,0:T(8,128)S(1)} %select_maximum_fusion), channel_id=1, source_target_pairs={{0,4},{4,0},{8,12},{12,8},{16,20},{20,16},{24,28},{28,24},{1,5},{5... | collective-permute-start | bytes 245768 | tf_op jit(solution)/shard_map/ppermute | solution.py:24
where the time goes:
time: 208 us; the launch traced here: 207 us
  blocking collectives  60.9 us (29%)
  waiting for transfers between devices  60.2 us (29%)
  starting transfers between devices  52.3 us (25%)
  other arithmetic  16.7 us (8%)
  matrix products  13.1 us (6%)
  local copies, waits for them, and re-layouts  2.43 us (1%)
    all_gather x1, blocking collectives, body(): every = lax.all_gather(sent, 'dp', axis=1)  50.9 us
    all_to_all x1, waiting for transfers between devices, body(): got = lax.all_to_all(packed, 'dp', 0, 0, axis_index_groups=SAME_PARITY)  28.7 us
    all_to_all x2, waiting for transfers between devices, exchange(): return lax.all_to_all(a, PLANE, 0, 0, axis_index_groups=SAME_CORE)  26.5 us
    ppermute x4, starting transfers between devices, swap_cores(): return lax.ppermute(a, 'tensor', CORE_PAIRS)  26.4 us
    all_to_all x2, starting transfers between devices, exchange(): return lax.all_to_all(a, PLANE, 0, 0, axis_index_groups=SAME_CORE)  11.3 us
    all_to_all x1, blocking collectives, exchange(): return lax.all_to_all(a, PLANE, 0, 0, axis_index_groups=SAME_CORE)  9.96 us
    all_to_all x1, starting transfers between devices, body(): got = lax.all_to_all(packed, 'dp', 0, 0, axis_index_groups=SAME_PARITY)  9.38 us
    dot_general x2, matrix products, joined_part(): jnp.dot(block, fc_weight, preferred_element_type=f32) * (PARTIAL / UP)  7.38 us
  transfers between devices with their start and end apart: 9, of which 6 were waited for; matrix products, arithmetic and copies ran while one was open for 4% of the time, Pallas kernels for 0%

commit v1 on v0

--- a/solution.py
+++ b/solution.py
@@ -96,12 +96,13 @@
         return lax.ppermute(values, "dp", [(i, (i + by) % Z) for i in range(Z)])
 
     arrived = through(head_weight, 1), through(head_other, -1)
+    near = [partial(parity, weight) for weight in (head_weight, head_other)]
     sums, sum_squares = [], []
-    for weight, got in zip((head_weight, head_other), arrived):
+    for own, got in zip(lax.optimization_barrier(near), arrived):
         got_square = squares(got, count)
         both = near_square + got_square
         here, there = lax.rsqrt(both) * (1.0 / SCALED), jnp.sqrt(got_square / both)
-        got = partial(parity, weight) * here[:, None] + got[:count].astype(f32) * there[:, None]
+        got = own * here[:, None] + got[:count].astype(f32) * there[:, None]
         sums.append(got.astype(f16).reshape(-1, half, width))
         sum_squares.append(both.reshape(-1, half))
     packed = sums + [levels(jnp.concatenate(sum_squares, axis=1), width)]
@@ -121,19 +122,14 @@
     own_top = jnp.max(logits, axis=(0, 2))
     own_total = jnp.sum(jnp.exp(logits - own_top[None, :, None]), axis=(0, 2))
     own = jnp.pad(jnp.stack([own_top, own_total, own_pick]), ((0, 5), (0, 128 - half)))
-    every = exchange(jnp.broadcast_to(own, (PEERS,) + own.shape))[:, :, :half]
-    top = jnp.max(every[:, 0], axis=0)
-    total = jnp.sum(every[:, 1] * jnp.exp(every[:, 0] - top), axis=0)
-    picked = jnp.sum(every[:, 2], axis=0)
-    lse = top + jnp.log(total)
-    logprob = logits - lse[None, :, None]
-    picked = picked - lse
-    away = jnp.concatenate([logprob[1], jnp.pad(picked[None], ((0, 7), (0, width - half)))])
-    got = swap_cores(away)
-    return (
-        by_core(core, logprob[0], got[:half]),
-        by_core(core, picked, got[half, :half]),
-    )
+    logits = by_core(core, logits[0], swap_cores(logits[1]))
+    every = lax.all_to_all(jnp.broadcast_to(own, (2 * PEERS,) + own.shape), PLANE, 0, 0)
+    every = every[:, :3, :half].reshape(4, 2, 4, 3, half)
+    top = jnp.max(every[:, :, :, 0], axis=(0, 2))
+    total = every[:, :, :, 1] * jnp.exp(every[:, :, :, 0] - top[None, :, None])
+    lse = (top + jnp.log(jnp.sum(total, axis=(0, 2)))).reshape(rows)
+    picked = jnp.sum(every[:, :, :, 2], axis=(0, 2)).reshape(rows)
+    return (logits - lse[:, None], picked - lse)
 
 
 def solution(mesh):

time: 208 us -> 205 us (0.986)
  blocking collectives: 60.9 us -> 50.9 us
  starting transfers between devices: 52.3 us -> 55.4 us
  other arithmetic: 16.7 us -> 19.2 us
    all_to_all x0 -> x1, starting transfers between devices: none -> 12.1 us  [body(): lax.all_to_all(jnp.broadcast_to(own, (2 * PEERS,) + own.shape), PLANE, 0, 0)]
    all_to_all x1 -> x0, blocking collectives: 9.96 us -> none  [exchange(): return lax.all_to_all(a, PLANE, 0, 0, axis_index_groups=SAME_CORE)]
    ppermute x4, starting transfers between devices: 26.4 us -> 18.4 us  [swap_cores(): return lax.ppermute(a, 'tensor', CORE_PAIRS)]
    all_to_all x0 -> x1, waiting for transfers between devices: none -> 4.81 us  [body(): lax.all_to_all(jnp.broadcast_to(own, (2 * PEERS,) + own.shape), PLANE, 0, 0)]
    ppermute x2, waiting for transfers between devices: 4.16 us -> 0.01 us  [through(): return lax.ppermute(values, 'dp', [(i, (i + by) % Z) for i in range(Z)])]
    convert_element_type x0 -> x2, other arithmetic: none -> 2.53 us  [body(): sums.append(got.astype(f16).reshape(-1, half, width))]
  transfers between devices with their start and end apart: 9 -> 10, of which waited for: 6 -> 4; matrix products, arithmetic and copies ran while one was open for 4% -> 7% of each run, Pallas kernels for 0% -> 0%
where the time goes in v1:
time: 205 us; the launch traced here: 204 us
  waiting for transfers between devices  58.7 us (29%)
  starting transfers between devices  55.4 us (27%)
  blocking collectives  50.9 us (25%)
  other arithmetic  19.2 us (9%)
  matrix products  14.7 us (7%)
  local copies, waits for them, and re-layouts  3.86 us (2%)
    all_gather x1, blocking collectives, body(): every = lax.all_gather(sent, 'dp', axis=1)  50.9 us
    all_to_all x1, waiting for transfers between devices, body(): got = lax.all_to_all(packed, 'dp', 0, 0, axis_index_groups=SAME_PARITY)  27.4 us
    all_to_all x2, waiting for transfers between devices, exchange(): return lax.all_to_all(a, PLANE, 0, 0, axis_index_groups=SAME_CORE)  26.5 us
    ppermute x4, starting transfers between devices, swap_cores(): return lax.ppermute(a, 'tensor', CORE_PAIRS)  18.4 us
    all_to_all x1, starting transfers between devices, body(): lax.all_to_all(jnp.broadcast_to(own, (2 * PEERS,) + own.shape), PLANE, 0, 0)  12.1 us
    all_to_all x2, starting transfers between devices, exchange(): return lax.all_to_all(a, PLANE, 0, 0, axis_index_groups=SAME_CORE)  11.3 us
    all_to_all x1, starting transfers between devices, body(): got = lax.all_to_all(packed, 'dp', 0, 0, axis_index_groups=SAME_PARITY)  8.4 us
    dot_general x2, matrix products, joined_part(): jnp.dot(block, fc_weight, preferred_element_type=f32) * (PARTIAL / UP)  7.38 us
  transfers between devices with their start and end apart: 10, of which 4 were waited for; matrix products, arithmetic and copies ran while one was open for 7% of the time, Pallas kernels for 0%

profile of v1, /device:TPU:65, one launch (start us, length us, event | category | flops | bytes accessed | tf_op | source)
XLA Modules:
  0.0 203.6 jit_solution(4051884857635085685)
XLA Ops:
  0.7 1.1 multiply_convert_fusion.1
  1.8 50.9 %all-gather.1 = f16[2,16,32,1536]{3,2,1,0:T(8,128)(2,1)} all-gather(f16[2,1,32,1536]{3,2,1,0:T(8,128)(2,1)S(1)} %bitcast.64), channel_id=1, replica_groups=mesh['dp'=16,'tensor'=8,'vocab'=4] {'dp'}, dimensions={1}, use_global_device_ids=true | all-gather | bytes 3342336 | tf_op jit(solution)/shard_map/all_gather | solution.py:64
  52.7 4.2 %multiply_convert_fusion = f16[16,32,1024]{2,1,0:T(8,128)(2,1)} fusion(bf16[1536,1024]{1,0:T(8,128)(2,1)S(1)} %copy-done, f16[2,16,32,1536]{3,2,1,0:T(8,128)(2,1)} %all-gather.1, s32[]{:T(128)S(6)} %select_n.52), kind=kOutput, calls=%fused_computation.7 | convolution fusion | flops 1612447744 | bytes 5767172 | tf_op jit(solution)/shard_map/dot_general | solution.py:68
  56.9 10.6 %collective-permute-start = (f16[16,32,1024]{2,1,0:T(8,128)(2,1)}, f16[16,32,1024]{2,1,0:T(8,128)(2,1)}, u32[]{:S(2)}, u32[]{:S(2)}) collective-permute-start(f16[16,32,1024]{2,1,0:T(8,128)(2,1)} %multiply_convert_fusion), channel_id=1, source_target_pairs={{0,4},{4,0},{8,12},{12,8},{16,20},{20,16},{24,28},{28,24},{1,5},{5... | collective-permute-start | bytes 3145736 | tf_op jit(solution)/shard_map/ppermute | solution.py:24
  67.5 3.2 %fusion.4 = f32[16,32,1024]{2,1,0:T(8,128)S(1)} fusion(bf16[1536,1024]{1,0:T(8,128)(2,1)S(1)} %copy-done, f16[2,16,32,1536]{3,2,1,0:T(8,128)(2,1)} %all-gather.1, s32[]{:T(128)S(6)} %select_n.51), kind=kOutput, calls=%fused_computation.8 | convolution fusion | flops 1611923456 | bytes 6815748 | tf_op jit(solution)/shard_map/dot_general | solution.py:68
  70.8 2.6 %add_convert_fusion = f16[16,32,1024]{2,1,0:T(8,128)(2,1)} fusion(f32[16,32,1024]{2,1,0:T(8,128)S(1)} %fusion.4, f16[16,32,1024]{2,1,0:T(8,128)(2,1)} %collective-permute-done), kind=kLoop, calls=%fused_computation.6 | loop fusion | flops 1572864 | bytes 4194304 | tf_op jit(solution)/shard_map/convert_element_type | solution.py:72
  73.4 6.9 %all-to-all-start = ((f16[16,32,1024]{2,1,0:T(8,128)(2,1)}), f16[16,32,1024]{2,1,0:T(8,128)(2,1)}, u32[]{:S(2)}, u32[]{:S(2)}) async-start(f16[16,32,1024]{2,1,0:T(8,128)(2,1)} %add_convert_fusion), calls=%async_computation | async-start | bytes 2097152 | tf_op jit(solution)/shard_map/all_to_all | solution.py:34
  80.4 17.0 %all-to-all-done = f16[16,32,1024]{2,1,0:T(8,128)(2,1)} async-done(((f16[16,32,1024]{2,1,0:T(8,128)(2,1)}), f16[16,32,1024]{2,1,0:T(8,128)(2,1)}, u32[]{:S(2)}, u32[]{:S(2)}) %all-to-all-start) | async-done | bytes 1048608 | tf_op jit(solution)/shard_map/all_to_all | solution.py:34
  97.4 1.4 convert_reduce_fusion
  98.8 1.1 broadcast_in_dim.7
  100.0 4.3 %all-to-all-start.1 = ((f16[16,32,1024]{2,1,0:T(8,128)(2,1)}), f16[16,32,1024]{2,1,0:T(8,128)(2,1)}, u32[]{:S(2)}, u32[]{:S(2)}) async-start(f16[16,32,1024]{2,1,0:T(8,128)(2,1)} %broadcast_in_dim.7), calls=%async_computation.1 | async-start | bytes 2097152 | tf_op jit(solution)/shard_map/all_to_all | solution.py:34
  104.3 3.7 %collective-permute-start.2 = (s32[512]{0:T(512)S(1)}, s32[512]{0:T(512)S(1)}, u32[]{:S(2)}, u32[]{:S(2)}) collective-permute-start(s32[512]{0:T(512)S(1)} %copy-done.4), channel_id=1, source_target_pairs={{0,4},{4,0},{8,12},{12,8},{16,20},{20,16},{24,28},{28,24},{1,5},{5... | collective-permute-start | bytes 6152 | tf_op jit(solution)/shard_map/ppermute | solution.py:24
  108.0 1.9 collective-permute-start.1
  110.0 9.4 %all-to-all-done.1 = f16[16,32,1024]{2,1,0:T(8,128)(2,1)} async-done(((f16[16,32,1024]{2,1,0:T(8,128)(2,1)}), f16[16,32,1024]{2,1,0:T(8,128)(2,1)}, u32[]{:S(2)}, u32[]{:S(2)}) %all-to-all-start.1) | async-done | bytes 1048608 | tf_op jit(solution)/shard_map/all_to_all | solution.py:34
  119.4 1.6 multiply_reduce_fusion
  121.2 2.4 %dynamic-slice_convert_fusion.1 = (bf16[8,1,32,1024]{3,2,1,0:T(8,128)(2,1)}, bf16[8,1,32,1024]{3,2,1,0:T(8,128)(2,1)S(1)}) fusion(f16[8,2,32,1024]{3,2,1,0:T(8,128)(2,1)} %bitcast.4, s32[]{:T(128)S(6)} %select_n.54, s32[]{:T(128)S(6)} %select_n.55), kind=kLoop, calls=%fused_computation.26 | loop fusion | flops 524288 | bytes 2097160 | tf_op jit(solution)/shard_map/convert_element_type | solution.py:85
  124.1 1.7 fusion.16
  125.7 0.9 pad_maximum_fusion.1
  126.6 1.9 collective-permute-start.3
  128.5 3.4 %collective-permute-start.4 = (f16[264,512]{1,0:T(8,128)(2,1)S(1)}, f16[264,512]{1,0:T(8,128)(2,1)}, u32[]{:S(2)}, u32[]{:S(2)}) collective-permute-start(f16[264,512]{1,0:T(8,128)(2,1)S(1)} %get-tuple-element.29), channel_id=1, source_target_pairs={{0,480},{32,0},{64,32},{96,64},{128,96},{160,128},{192,160},{224,1... | collective-permute-start | bytes 811016 | tf_op jit(solution)/shard_map/ppermute | solution.py:96
  131.9 2.7 %fusion.47 = f32[256,512]{1,0:T(8,128)} fusion(bf16[256,1024]{1,0:T(8,128)(2,1)} %bitcast.59, bf16[1024,512]{1,0:T(8,128)(2,1)} %param.10), kind=kOutput, calls=%fused_computation.100 | convolution fusion | flops 268435456 | bytes 2097152 | tf_op jit(solution)/shard_map/dot_general | solution.py:86
  134.6 2.5 %fusion.48 = f32[256,512]{1,0:T(8,128)} fusion(bf16[256,1024]{1,0:T(8,128)(2,1)S(1)} %bitcast.60, bf16[1024,512]{1,0:T(8,128)(2,1)} %collective-permute-done.1), kind=kOutput, calls=%fused_computation.101 | convolution fusion | flops 268435456 | bytes 2097152 | tf_op jit(solution)/shard_map/dot_general | solution.py:86
  137.7 1.4 fusion.42
  139.4 1.3 add_convert_fusion.2
  140.7 1.3 add_convert_fusion.1
  141.9 0.9 fusion.18
  142.9 8.4 %all-to-all-start.2 = ((f16[8,72,512]{2,1,0:T(8,128)(2,1)}), f16[8,72,512]{2,1,0:T(8,128)(2,1)}, u32[]{:S(2)}, u32[]{:S(2)}) async-start(f16[8,72,512]{2,1,0:T(8,128)(2,1)} %fusion.18), calls=%async_computation.2 | async-start | bytes 1179648 | tf_op jit(solution)/shard_map/all_to_all | solution.py:110
  151.4 27.4 %all-to-all-done.2 = f16[8,72,512]{2,1,0:T(8,128)(2,1)} async-done(((f16[8,72,512]{2,1,0:T(8,128)(2,1)}), f16[8,72,512]{2,1,0:T(8,128)(2,1)}, u32[]{:S(2)}, u32[]{:S(2)}) %all-to-all-start.2) | async-done | bytes 589856 | tf_op jit(solution)/shard_map/all_to_all | solution.py:110
  179.7 1.3 multiply_reduce_fusion.1
  182.4 12.1 %all-to-all-start.3 = ((f32[32,8,128]{2,1,0:T(8,128)}), f32[32,8,128]{2,1,0:T(8,128)S(1)}, u32[]{:S(2)}, u32[]{:S(2)}) async-start(f32[32,8,128]{2,1,0:T(8,128)} %broadcast_in_dim.9), calls=%async_computation.3 | async-start | bytes 262144 | tf_op jit(solution)/shard_map/all_to_all | solution.py:126
  195.1 2.1 %collective-permute-start.5 = (f32[32,512]{1,0:T(8,128)}, f32[32,512]{1,0:T(8,128)S(1)}, u32[]{:S(2)}, u32[]{:S(2)}) collective-permute-start(f32[32,512]{1,0:T(8,128)} %get-tuple-element.25), channel_id=1, source_target_pairs={{0,4},{4,0},{8,12},{12,8},{16,20},{20,16},{24,28},{28,24},{1,5},{5... | collective-permute-start | bytes 196616 | tf_op jit(solution)/shard_map/ppermute | solution.py:24
  197.3 4.8 %all-to-all-done.3 = f32[32,8,128]{2,1,0:T(8,128)S(1)} async-done(((f32[32,8,128]{2,1,0:T(8,128)}), f32[32,8,128]{2,1,0:T(8,128)S(1)}, u32[]{:S(2)}, u32[]{:S(2)}) %all-to-all-start.3) | async-done | bytes 131104 | tf_op jit(solution)/shard_map/all_to_all | solution.py:126
  (65 shorter events, 6.2 us)
Async XLA Ops:
  0.6 52.1 %copy-start = (bf16[1536,1024]{1,0:T(8,128)(2,1)S(1)}, bf16[1536,1024]{1,0:T(8,128)(2,1)}, u32[]{:S(2)}) copy-start(bf16[1536,1024]{1,0:T(8,128)(2,1)} %param.8) | copy-start | bytes 9437188
  56.9 13.9 %collective-permute-start = (f16[16,32,1024]{2,1,0:T(8,128)(2,1)}, f16[16,32,1024]{2,1,0:T(8,128)(2,1)}, u32[]{:S(2)}, u32[]{:S(2)}) collective-permute-start(f16[16,32,1024]{2,1,0:T(8,128)(2,1)} %multiply_convert_fusion), channel_id=1, source_target_pairs={{0,4},{4,0},{8,12},{12,8},{16,20},{20,16},{24,28},{28,24},{1,5},{5... | collective-permute-start | bytes 3145736 | tf_op jit(solution)/shard_map/ppermute | solution.py:24
  73.4 7.0 %copy-start.3 = (f32[1024]{0:T(1024)S(1)}, f32[1024]{0:T(1024)}, u32[]{:S(2)}) copy-start(f32[1024]{0:T(1024)} %param.9) | copy-start | bytes 12292
  73.4 24.0 %all-to-all-start = ((f16[16,32,1024]{2,1,0:T(8,128)(2,1)}), f16[16,32,1024]{2,1,0:T(8,128)(2,1)}, u32[]{:S(2)}, u32[]{:S(2)}) async-start(f16[16,32,1024]{2,1,0:T(8,128)(2,1)} %add_convert_fusion), calls=%async_computation | async-start | bytes 2097152 | tf_op jit(solution)/shard_map/all_to_all | solution.py:34
  80.4 24.0 %copy-start.4 = (s32[512]{0:T(512)S(1)}, s32[512]{0:T(512)}, u32[]{:S(2)}) copy-start(s32[512]{0:T(512)} %param.11) | copy-start | bytes 6148
  100.0 19.5 %all-to-all-start.1 = ((f16[16,32,1024]{2,1,0:T(8,128)(2,1)}), f16[16,32,1024]{2,1,0:T(8,128)(2,1)}, u32[]{:S(2)}, u32[]{:S(2)}) async-start(f16[16,32,1024]{2,1,0:T(8,128)(2,1)} %broadcast_in_dim.7), calls=%async_computation.1 | async-start | bytes 2097152 | tf_op jit(solution)/shard_map/all_to_all | solution.py:34
  104.3 5.6 %collective-permute-start.2 = (s32[512]{0:T(512)S(1)}, s32[512]{0:T(512)S(1)}, u32[]{:S(2)}, u32[]{:S(2)}) collective-permute-start(s32[512]{0:T(512)S(1)} %copy-done.4), channel_id=1, source_target_pairs={{0,4},{4,0},{8,12},{12,8},{16,20},{20,16},{24,28},{28,24},{1,5},{5... | collective-permute-start | bytes 6152 | tf_op jit(solution)/shard_map/ppermute | solution.py:24
  108.0 16.0 %collective-permute-start.1 = (bf16[1024,512]{1,0:T(8,128)(2,1)}, bf16[1024,512]{1,0:T(8,128)(2,1)}, u32[]{:S(2)}, u32[]{:S(2)}) collective-permute-start(bf16[1024,512]{1,0:T(8,128)(2,1)} %param.10), channel_id=1, source_target_pairs={{0,4},{4,0},{8,12},{12,8},{16,20},{20,16},{24,28},{28,24},{1,5},{5... | collective-permute-start | bytes 3145736 | tf_op jit(solution)/shard_map/ppermute | solution.py:24
  121.2 2.4 %copy-start.2 = (bf16[1024,512]{1,0:T(8,128)(2,1)S(1)}, bf16[1024,512]{1,0:T(8,128)(2,1)}, u32[]{:S(2)}) copy-start(bf16[1024,512]{1,0:T(8,128)(2,1)} %param.10) | copy-start | bytes 3145732
  126.6 10.6 %collective-permute-start.3 = (f16[264,512]{1,0:T(8,128)(2,1)}, f16[264,512]{1,0:T(8,128)(2,1)}, u32[]{:S(2)}, u32[]{:S(2)}) collective-permute-start(f16[264,512]{1,0:T(8,128)(2,1)} %get-tuple-element.28), channel_id=1, source_target_pairs={{0,32},{32,64},{64,96},{96,128},{128,160},{160,192},{192,224},{224... | collective-permute-start | bytes 811016 | tf_op jit(solution)/shard_map/ppermute | solution.py:96
  128.5 8.6 %collective-permute-start.4 = (f16[264,512]{1,0:T(8,128)(2,1)S(1)}, f16[264,512]{1,0:T(8,128)(2,1)}, u32[]{:S(2)}, u32[]{:S(2)}) collective-permute-start(f16[264,512]{1,0:T(8,128)(2,1)S(1)} %get-tuple-element.29), channel_id=1, source_target_pairs={{0,480},{32,0},{64,32},{96,64},{128,96},{160,128},{192,160},{224,1... | collective-permute-start | bytes 811016 | tf_op jit(solution)/shard_map/ppermute | solution.py:96
  131.9 2.7 %copy-start.1 = (bf16[8,1,32,1024]{3,2,1,0:T(8,128)(2,1)S(1)}, bf16[8,1,32,1024]{3,2,1,0:T(8,128)(2,1)}, u32[]{:S(2)}) copy-start(bf16[8,1,32,1024]{3,2,1,0:T(8,128)(2,1)} %get-tuple-element.22) | copy-start | bytes 1572868
  139.4 11.9 %copy-start.5 = (s32[64]{0:T(128)S(1)}, s32[64]{0:T(128)}, u32[]{:S(2)}) copy-start(s32[64]{0:T(128)} %param.12) | copy-start | bytes 772
  142.9 35.9 %all-to-all-start.2 = ((f16[8,72,512]{2,1,0:T(8,128)(2,1)}), f16[8,72,512]{2,1,0:T(8,128)(2,1)}, u32[]{:S(2)}, u32[]{:S(2)}) async-start(f16[8,72,512]{2,1,0:T(8,128)(2,1)} %fusion.18), calls=%async_computation.2 | async-start | bytes 1179648 | tf_op jit(solution)/shard_map/all_to_all | solution.py:110
  182.4 19.7 %all-to-all-start.3 = ((f32[32,8,128]{2,1,0:T(8,128)}), f32[32,8,128]{2,1,0:T(8,128)S(1)}, u32[]{:S(2)}, u32[]{:S(2)}) async-start(f32[32,8,128]{2,1,0:T(8,128)} %broadcast_in_dim.9), calls=%async_computation.3 | async-start | bytes 262144 | tf_op jit(solution)/shard_map/all_to_all | solution.py:126
  195.1 7.8 %collective-permute-start.5 = (f32[32,512]{1,0:T(8,128)}, f32[32,512]{1,0:T(8,128)S(1)}, u32[]{:S(2)}, u32[]{:S(2)}) collective-permute-start(f32[32,512]{1,0:T(8,128)} %get-tuple-element.25), channel_id=1, source_target_pairs={{0,4},{4,0},{8,12},{12,8},{16,20},{20,16},{24,28},{28,24},{1,5},{5... | collective-permute-start | bytes 196616 | tf_op jit(solution)/shard_map/ppermute | solution.py:24

commit v2 on v1

--- a/solution.py
+++ b/solution.py
@@ -9,7 +9,6 @@
 
 UP = 2.0**9
 PARTIAL = 2.0**-2
-SCALED = 2.0**-7
 LEVEL = 2.0**-7
 FINE = 2.0**11
 
@@ -73,38 +72,36 @@
     later = lax.optimization_barrier((head_weight, draft_map, chip))
     head_other, map_other = swap_cores(later[0]), swap_cores(later[1])
     joined = jnp.sum(exchange(chip).astype(f32), axis=0)
-    scaled = (joined * (norm_gain * (SCALED / PARTIAL))).astype(f16)
+    scaled = (joined * (norm_gain * (1.0 / PARTIAL))).astype(bf16)
     scaled = exchange(jnp.broadcast_to(scaled, (PEERS,) + scaled.shape))
 
     gain = lax.optimization_barrier((norm_gain, map_other))[0]
-    own = scaled.astype(f32) * (1.0 / (gain * SCALED))
+    own = scaled.astype(f32) * (1.0 / gain)
     square = (jnp.mean(own * own, axis=2) + eps).reshape(Z // 2, 2, half)
     scaled = scaled.reshape(Z // 2, 2, half, depth)
 
     def partial(h, weight):
-        block = pick(scaled, h).astype(bf16).reshape(-1, depth)
-        return jnp.dot(block, weight, preferred_element_type=f32)
+        block = pick(scaled, h).reshape(-1, depth)
+        return jnp.dot(block, weight, preferred_element_type=f32).reshape(-1, half, width)
 
-    far_square = pick(square, 1 - parity).reshape(-1)
-    near_square = pick(square, parity).reshape(-1)
+    far_square, near_square = pick(square, 1 - parity), pick(square, parity)
     far_level = levels(far_square, width)
-    count = far_square.shape[0]
 
     def through(weight, by):
-        values = partial(1 - parity, weight) * (lax.rsqrt(far_square) * (1.0 / SCALED))[:, None]
-        values = jnp.concatenate([values.astype(f16), far_level])
+        values = partial(1 - parity, weight) * lax.rsqrt(far_square)[:, :, None]
+        values = jnp.concatenate([values.astype(f16), far_level], axis=1)
         return lax.ppermute(values, "dp", [(i, (i + by) % Z) for i in range(Z)])
 
     arrived = through(head_weight, 1), through(head_other, -1)
     near = [partial(parity, weight) for weight in (head_weight, head_other)]
     sums, sum_squares = [], []
     for own, got in zip(lax.optimization_barrier(near), arrived):
-        got_square = squares(got, count)
+        got_square = squares(got, half)
         both = near_square + got_square
-        here, there = lax.rsqrt(both) * (1.0 / SCALED), jnp.sqrt(got_square / both)
-        got = own * here[:, None] + got[:count].astype(f32) * there[:, None]
-        sums.append(got.astype(f16).reshape(-1, half, width))
-        sum_squares.append(both.reshape(-1, half))
+        here, there = lax.rsqrt(both), jnp.sqrt(got_square / both)
+        got = own * here[:, :, None] + got[:, :half].astype(f32) * there[:, :, None]
+        sums.append(got.astype(f16))
+        sum_squares.append(both)
     packed = sums + [levels(jnp.concatenate(sum_squares, axis=1), width)]
     packed = jnp.concatenate(packed, axis=1)
     got = lax.all_to_all(packed, "dp", 0, 0, axis_index_groups=SAME_PARITY)

time: 205 us -> 204 us (level)
  other arithmetic: 19.2 us -> 14 us
  local copies, waits for them, and re-layouts: 3.86 us -> 6.17 us
    convert_element_type x4 -> x2, other arithmetic: 4.92 us -> 1.96 us  [the longest x1 1.95 us: body(): sums.append(got.astype(f16))]
where the time goes in v2:
time: 204 us; the launch traced here: 203 us
  waiting for transfers between devices  60.2 us (30%)
  starting transfers between devices  55.3 us (27%)
  blocking collectives  50.9 us (25%)
  matrix products  15.8 us (8%)
  other arithmetic  14 us (7%)
  local copies, waits for them, and re-layouts  6.17 us (3%)
    all_gather x1, blocking collectives, body(): every = lax.all_gather(sent, 'dp', axis=1)  50.9 us
    all_to_all x1, waiting for transfers between devices, body(): got = lax.all_to_all(packed, 'dp', 0, 0, axis_index_groups=SAME_PARITY)  28.9 us
    all_to_all x2, waiting for transfers between devices, exchange(): return lax.all_to_all(a, PLANE, 0, 0, axis_index_groups=SAME_CORE)  26.5 us
    ppermute x4, starting transfers between devices, swap_cores(): return lax.ppermute(a, 'tensor', CORE_PAIRS)  18.4 us
    all_to_all x2, starting transfers between devices, exchange(): return lax.all_to_all(a, PLANE, 0, 0, axis_index_groups=SAME_CORE)  11.3 us
    all_to_all x1, starting transfers between devices, body(): lax.all_to_all(jnp.broadcast_to(own, (2 * PEERS,) + own.shape), PLANE, 0, 0)  11.2 us
    all_to_all x1, starting transfers between devices, body(): got = lax.all_to_all(packed, 'dp', 0, 0, axis_index_groups=SAME_PARITY)  9.18 us
    dot_general x4, matrix products, partial(): jnp.dot(block, weight, preferred_element_type=f32).reshape(-1, half, width)  8.41 us
  transfers between devices with their start and end apart: 10, of which 4 were waited for; matrix products, arithmetic and copies ran while one was open for 7% of the time, Pallas kernels for 0%

profile of v2, /device:TPU:65, one launch (start us, length us, event | category | flops | bytes accessed | tf_op | source)
XLA Modules:
  0.0 203.3 jit_solution(15545528726209540638)
XLA Ops:
  0.7 1.1 multiply_convert_fusion.1
  1.8 50.9 %all-gather.1 = f16[2,16,32,1536]{3,2,1,0:T(8,128)(2,1)} all-gather(f16[2,1,32,1536]{3,2,1,0:T(8,128)(2,1)S(1)} %bitcast.84), channel_id=1, replica_groups=mesh['dp'=16,'tensor'=8,'vocab'=4] {'dp'}, dimensions={1}, use_global_device_ids=true | all-gather | bytes 3342336 | tf_op jit(solution)/shard_map/all_gather | solution.py:63
  52.7 4.2 %multiply_convert_fusion = f16[16,32,1024]{2,1,0:T(8,128)(2,1)} fusion(bf16[1536,1024]{1,0:T(8,128)(2,1)S(1)} %copy-done, f16[2,16,32,1536]{3,2,1,0:T(8,128)(2,1)} %all-gather.1, s32[]{:T(128)S(6)} %select_n.52), kind=kOutput, calls=%fused_computation.7 | convolution fusion | flops 1612447744 | bytes 5767172 | tf_op jit(solution)/shard_map/dot_general | solution.py:67
  56.9 10.6 %collective-permute-start = (f16[16,32,1024]{2,1,0:T(8,128)(2,1)}, f16[16,32,1024]{2,1,0:T(8,128)(2,1)}, u32[]{:S(2)}, u32[]{:S(2)}) collective-permute-start(f16[16,32,1024]{2,1,0:T(8,128)(2,1)} %multiply_convert_fusion), channel_id=1, source_target_pairs={{0,4},{4,0},{8,12},{12,8},{16,20},{20,16},{24,28},{28,24},{1,5},{5... | collective-permute-start | bytes 3145736 | tf_op jit(solution)/shard_map/ppermute | solution.py:23
  67.5 3.2 %fusion.4 = f32[16,32,1024]{2,1,0:T(8,128)S(1)} fusion(bf16[1536,1024]{1,0:T(8,128)(2,1)S(1)} %copy-done, f16[2,16,32,1536]{3,2,1,0:T(8,128)(2,1)} %all-gather.1, s32[]{:T(128)S(6)} %select_n.51), kind=kOutput, calls=%fused_computation.8 | convolution fusion | flops 1611923456 | bytes 6815748 | tf_op jit(solution)/shard_map/dot_general | solution.py:67
  70.8 2.6 %add_convert_fusion = f16[16,32,1024]{2,1,0:T(8,128)(2,1)} fusion(f32[16,32,1024]{2,1,0:T(8,128)S(1)} %fusion.4, f16[16,32,1024]{2,1,0:T(8,128)(2,1)} %collective-permute-done), kind=kLoop, calls=%fused_computation.6 | loop fusion | flops 1572864 | bytes 4194304 | tf_op jit(solution)/shard_map/convert_element_type | solution.py:71
  73.4 6.9 %all-to-all-start = ((f16[16,32,1024]{2,1,0:T(8,128)(2,1)}), f16[16,32,1024]{2,1,0:T(8,128)(2,1)}, u32[]{:S(2)}, u32[]{:S(2)}) async-start(f16[16,32,1024]{2,1,0:T(8,128)(2,1)} %add_convert_fusion), calls=%async_computation | async-start | bytes 2097152 | tf_op jit(solution)/shard_map/all_to_all | solution.py:33
  80.4 17.0 %all-to-all-done = f16[16,32,1024]{2,1,0:T(8,128)(2,1)} async-done(((f16[16,32,1024]{2,1,0:T(8,128)(2,1)}), f16[16,32,1024]{2,1,0:T(8,128)(2,1)}, u32[]{:S(2)}, u32[]{:S(2)}) %all-to-all-start) | async-done | bytes 1048608 | tf_op jit(solution)/shard_map/all_to_all | solution.py:33
  97.4 1.4 convert_reduce_fusion
  98.8 1.1 broadcast_in_dim.7
  100.0 4.3 %all-to-all-start.1 = ((bf16[16,32,1024]{2,1,0:T(8,128)(2,1)}), bf16[16,32,1024]{2,1,0:T(8,128)(2,1)}, u32[]{:S(2)}, u32[]{:S(2)}) async-start(bf16[16,32,1024]{2,1,0:T(8,128)(2,1)} %broadcast_in_dim.7), calls=%async_computation.1 | async-start | bytes 2097152 | tf_op jit(solution)/shard_map/all_to_all | solution.py:33
  104.3 3.7 %collective-permute-start.2 = (s32[512]{0:T(512)S(1)}, s32[512]{0:T(512)S(1)}, u32[]{:S(2)}, u32[]{:S(2)}) collective-permute-start(s32[512]{0:T(512)S(1)} %copy-done.4), channel_id=1, source_target_pairs={{0,4},{4,0},{8,12},{12,8},{16,20},{20,16},{24,28},{28,24},{1,5},{5... | collective-permute-start | bytes 6152 | tf_op jit(solution)/shard_map/ppermute | solution.py:23
  108.0 1.9 collective-permute-start.1
  110.0 9.4 %all-to-all-done.1 = bf16[16,32,1024]{2,1,0:T(8,128)(2,1)} async-done(((bf16[16,32,1024]{2,1,0:T(8,128)(2,1)}), bf16[16,32,1024]{2,1,0:T(8,128)(2,1)}, u32[]{:S(2)}, u32[]{:S(2)}) %all-to-all-start.1) | async-done | bytes 1048608 | tf_op jit(solution)/shard_map/all_to_all | solution.py:33
  119.4 1.6 multiply_reduce_fusion
  121.1 1.1 dynamic-slice_bitcast_fusion
  122.2 1.7 fusion.15
  123.9 1.8 fusion.16
  125.9 1.9 collective-permute-start.3
  127.8 3.4 %collective-permute-start.4 = (f16[8,40,512]{2,0,1:T(8,128)(2,1)S(1)}, f16[8,40,512]{2,0,1:T(8,128)(2,1)S(1)}, u32[]{:S(2)}, u32[]{:S(2)}) collective-permute-start(f16[8,40,512]{2,0,1:T(8,128)(2,1)S(1)} %get-tuple-element.23), channel_id=1, source_target_pairs={{0,480},{32,0},{64,32},{96,64},{128,96},{160,128},{192,160},{224,1... | collective-permute-start | bytes 983048 | tf_op jit(solution)/shard_map/ppermute | solution.py:93
  131.2 2.3 %fusion.21 = f32[8,32,512]{2,1,0:T(8,128)} fusion(bf16[1024,512]{1,0:T(8,128)(2,1)S(1)} %copy-done.1, bf16[8,2,32,1024]{3,2,1,0:T(8,128)(2,1)} %bitcast.4, s32[]{:T(128)S(6)} %select_n.54), kind=kOutput, calls=%fused_computation.23 | convolution fusion | flops 268435456 | bytes 2097156 | tf_op jit(solution)/shard_map/dot_general | solution.py:85
  133.5 2.6 %fusion.18 = f32[8,32,512]{2,1,0:T(8,128)} fusion(bf16[1024,512]{1,0:T(8,128)(2,1)} %collective-permute-done.1, bf16[8,2,32,1024]{3,2,1,0:T(8,128)(2,1)} %bitcast.4, s32[]{:T(128)S(6)} %select_n.54), kind=kOutput, calls=%fused_computation.20 | convolution fusion | flops 268435456 | bytes 2097156 | tf_op jit(solution)/shard_map/dot_general | solution.py:85
  137.9 1.9 fusion.26
  140.1 1.0 copy.113
  141.1 9.2 %all-to-all-start.2 = ((f16[8,72,512]{2,1,0:T(8,128)(2,1)}), f16[8,72,512]{2,1,0:T(8,128)(2,1)}, u32[]{:S(2)}, u32[]{:S(2)}) async-start(f16[8,72,512]{2,1,0:T(8,128)(2,1)} %copy.113), calls=%async_computation.2 | async-start | bytes 1179648 | tf_op jit(solution)/shard_map/all_to_all | solution.py:107
  150.5 28.9 %all-to-all-done.2 = f16[8,72,512]{2,1,0:T(8,128)(2,1)} async-done(((f16[8,72,512]{2,1,0:T(8,128)(2,1)}), f16[8,72,512]{2,1,0:T(8,128)(2,1)}, u32[]{:S(2)}, u32[]{:S(2)}) %all-to-all-start.2) | async-done | bytes 589856 | tf_op jit(solution)/shard_map/all_to_all | solution.py:107
  179.4 0.8 fusion.66
  180.2 1.3 multiply_reduce_fusion.1
  183.0 11.2 %all-to-all-start.3 = ((f32[32,8,128]{2,1,0:T(8,128)}), f32[32,8,128]{2,1,0:T(8,128)S(1)}, u32[]{:S(2)}, u32[]{:S(2)}) async-start(f32[32,8,128]{2,1,0:T(8,128)} %broadcast_in_dim.9), calls=%async_computation.3 | async-start | bytes 262144 | tf_op jit(solution)/shard_map/all_to_all | solution.py:123
  194.8 2.1 %collective-permute-start.5 = (f32[32,512]{1,0:T(8,128)}, f32[32,512]{1,0:T(8,128)S(1)}, u32[]{:S(2)}, u32[]{:S(2)}) collective-permute-start(f32[32,512]{1,0:T(8,128)} %get-tuple-element.21), channel_id=1, source_target_pairs={{0,4},{4,0},{8,12},{12,8},{16,20},{20,16},{24,28},{28,24},{1,5},{5... | collective-permute-start | bytes 196616 | tf_op jit(solution)/shard_map/ppermute | solution.py:23
  197.0 4.8 %all-to-all-done.3 = f32[32,8,128]{2,1,0:T(8,128)S(1)} async-done(((f32[32,8,128]{2,1,0:T(8,128)}), f32[32,8,128]{2,1,0:T(8,128)S(1)}, u32[]{:S(2)}, u32[]{:S(2)}) %all-to-all-start.3) | async-done | bytes 131104 | tf_op jit(solution)/shard_map/all_to_all | solution.py:123
  202.6 0.7 fusion.39
  (62 shorter events, 5.4 us)
Async XLA Ops:
  0.6 52.1 %copy-start = (bf16[1536,1024]{1,0:T(8,128)(2,1)S(1)}, bf16[1536,1024]{1,0:T(8,128)(2,1)}, u32[]{:S(2)}) copy-start(bf16[1536,1024]{1,0:T(8,128)(2,1)} %param.8) | copy-start | bytes 9437188
  56.9 13.9 %collective-permute-start = (f16[16,32,1024]{2,1,0:T(8,128)(2,1)}, f16[16,32,1024]{2,1,0:T(8,128)(2,1)}, u32[]{:S(2)}, u32[]{:S(2)}) collective-permute-start(f16[16,32,1024]{2,1,0:T(8,128)(2,1)} %multiply_convert_fusion), channel_id=1, source_target_pairs={{0,4},{4,0},{8,12},{12,8},{16,20},{20,16},{24,28},{28,24},{1,5},{5... | collective-permute-start | bytes 3145736 | tf_op jit(solution)/shard_map/ppermute | solution.py:23
  73.4 7.0 %copy-start.3 = (f32[1024]{0:T(1024)S(1)}, f32[1024]{0:T(1024)}, u32[]{:S(2)}) copy-start(f32[1024]{0:T(1024)} %param.9) | copy-start | bytes 12292
  73.4 24.0 %all-to-all-start = ((f16[16,32,1024]{2,1,0:T(8,128)(2,1)}), f16[16,32,1024]{2,1,0:T(8,128)(2,1)}, u32[]{:S(2)}, u32[]{:S(2)}) async-start(f16[16,32,1024]{2,1,0:T(8,128)(2,1)} %add_convert_fusion), calls=%async_computation | async-start | bytes 2097152 | tf_op jit(solution)/shard_map/all_to_all | solution.py:33
  80.4 23.9 %copy-start.4 = (s32[512]{0:T(512)S(1)}, s32[512]{0:T(512)}, u32[]{:S(2)}) copy-start(s32[512]{0:T(512)} %param.11) | copy-start | bytes 6148
  100.0 19.5 %all-to-all-start.1 = ((bf16[16,32,1024]{2,1,0:T(8,128)(2,1)}), bf16[16,32,1024]{2,1,0:T(8,128)(2,1)}, u32[]{:S(2)}, u32[]{:S(2)}) async-start(bf16[16,32,1024]{2,1,0:T(8,128)(2,1)} %broadcast_in_dim.7), calls=%async_computation.1 | async-start | bytes 2097152 | tf_op jit(solution)/shard_map/all_to_all | solution.py:33
  104.3 5.6 %collective-permute-start.2 = (s32[512]{0:T(512)S(1)}, s32[512]{0:T(512)S(1)}, u32[]{:S(2)}, u32[]{:S(2)}) collective-permute-start(s32[512]{0:T(512)S(1)} %copy-done.4), channel_id=1, source_target_pairs={{0,4},{4,0},{8,12},{12,8},{16,20},{20,16},{24,28},{28,24},{1,5},{5... | collective-permute-start | bytes 6152 | tf_op jit(solution)/shard_map/ppermute | solution.py:23
  108.0 15.9 %collective-permute-start.1 = (bf16[1024,512]{1,0:T(8,128)(2,1)}, bf16[1024,512]{1,0:T(8,128)(2,1)}, u32[]{:S(2)}, u32[]{:S(2)}) collective-permute-start(bf16[1024,512]{1,0:T(8,128)(2,1)} %param.10), channel_id=1, source_target_pairs={{0,4},{4,0},{8,12},{12,8},{16,20},{20,16},{24,28},{28,24},{1,5},{5... | collective-permute-start | bytes 3145736 | tf_op jit(solution)/shard_map/ppermute | solution.py:23
  123.9 7.3 %copy-start.1 = (bf16[1024,512]{1,0:T(8,128)(2,1)S(1)}, bf16[1024,512]{1,0:T(8,128)(2,1)}, u32[]{:S(2)}) copy-start(bf16[1024,512]{1,0:T(8,128)(2,1)} %param.10) | copy-start | bytes 3145732
  125.9 10.2 %collective-permute-start.3 = (f16[8,40,512]{2,0,1:T(8,128)(2,1)S(1)}, f16[8,40,512]{2,0,1:T(8,128)(2,1)S(1)}, u32[]{:S(2)}, u32[]{:S(2)}) collective-permute-start(f16[8,40,512]{2,0,1:T(8,128)(2,1)S(1)} %get-tuple-element.22), channel_id=1, source_target_pairs={{0,32},{32,64},{64,96},{96,128},{128,160},{160,192},{192,224},{224... | collective-permute-start | bytes 983048 | tf_op jit(solution)/shard_map/ppermute | solution.py:93
  127.8 8.3 %collective-permute-start.4 = (f16[8,40,512]{2,0,1:T(8,128)(2,1)S(1)}, f16[8,40,512]{2,0,1:T(8,128)(2,1)S(1)}, u32[]{:S(2)}, u32[]{:S(2)}) collective-permute-start(f16[8,40,512]{2,0,1:T(8,128)(2,1)S(1)} %get-tuple-element.23), channel_id=1, source_target_pairs={{0,480},{32,0},{64,32},{96,64},{128,96},{160,128},{192,160},{224,1... | collective-permute-start | bytes 983048 | tf_op jit(solution)/shard_map/ppermute | solution.py:93
  136.1 0.7 copy-start.2
  139.9 10.4 %copy-start.5 = (s32[64]{0:T(128)S(1)}, s32[64]{0:T(128)}, u32[]{:S(2)}) copy-start(s32[64]{0:T(128)} %param.12) | copy-start | bytes 772
  141.1 38.3 %all-to-all-start.2 = ((f16[8,72,512]{2,1,0:T(8,128)(2,1)}), f16[8,72,512]{2,1,0:T(8,128)(2,1)}, u32[]{:S(2)}, u32[]{:S(2)}) async-start(f16[8,72,512]{2,1,0:T(8,128)(2,1)} %copy.113), calls=%async_computation.2 | async-start | bytes 1179648 | tf_op jit(solution)/shard_map/all_to_all | solution.py:107
  183.0 18.8 %all-to-all-start.3 = ((f32[32,8,128]{2,1,0:T(8,128)}), f32[32,8,128]{2,1,0:T(8,128)S(1)}, u32[]{:S(2)}, u32[]{:S(2)}) async-start(f32[32,8,128]{2,1,0:T(8,128)} %broadcast_in_dim.9), calls=%async_computation.3 | async-start | bytes 262144 | tf_op jit(solution)/shard_map/all_to_all | solution.py:123
  194.8 7.8 %collective-permute-start.5 = (f32[32,512]{1,0:T(8,128)}, f32[32,512]{1,0:T(8,128)S(1)}, u32[]{:S(2)}, u32[]{:S(2)}) collective-permute-start(f32[32,512]{1,0:T(8,128)} %get-tuple-element.21), channel_id=1, source_target_pairs={{0,4},{4,0},{8,12},{12,8},{16,20},{20,16},{24,28},{28,24},{1,5},{5... | collective-permute-start | bytes 196616 | tf_op jit(solution)/shard_map/ppermute | solution.py:23

commit v3 on v2

--- a/solution.py
+++ b/solution.py
@@ -75,31 +75,29 @@
     scaled = (joined * (norm_gain * (1.0 / PARTIAL))).astype(bf16)
     scaled = exchange(jnp.broadcast_to(scaled, (PEERS,) + scaled.shape))
 
-    gain = lax.optimization_barrier((norm_gain, map_other))[0]
+    head = jnp.concatenate([head_weight, head_other], axis=1)
+    gain, _, head = lax.optimization_barrier((norm_gain, map_other, head))
     own = scaled.astype(f32) * (1.0 / gain)
     square = (jnp.mean(own * own, axis=2) + eps).reshape(Z // 2, 2, half)
     scaled = scaled.reshape(Z // 2, 2, half, depth)
 
-    def partial(h, weight):
+    def partial(h):
         block = pick(scaled, h).reshape(-1, depth)
-        return jnp.dot(block, weight, preferred_element_type=f32).reshape(-1, half, width)
+        return jnp.dot(block, head, preferred_element_type=f32).reshape(-1, half, 2 * width)
 
     far_square, near_square = pick(square, 1 - parity), pick(square, parity)
+    far = (partial(1 - parity) * lax.rsqrt(far_square)[:, :, None]).astype(f16)
     far_level = levels(far_square, width)
-
-    def through(weight, by):
-        values = partial(1 - parity, weight) * lax.rsqrt(far_square)[:, :, None]
-        values = jnp.concatenate([values.astype(f16), far_level], axis=1)
-        return lax.ppermute(values, "dp", [(i, (i + by) % Z) for i in range(Z)])
-
-    arrived = through(head_weight, 1), through(head_other, -1)
-    near = [partial(parity, weight) for weight in (head_weight, head_other)]
+    near = lax.optimization_barrier(partial(parity))
     sums, sum_squares = [], []
-    for own, got in zip(lax.optimization_barrier(near), arrived):
+    for v, by in ((0, 1), (1, -1)):
+        part = slice(v * width, (v + 1) * width)
+        got = jnp.concatenate([far[:, :, part], far_level], axis=1)
+        got = lax.ppermute(got, "dp", [(i, (i + by) % Z) for i in range(Z)])
         got_square = squares(got, half)
         both = near_square + got_square
         here, there = lax.rsqrt(both), jnp.sqrt(got_square / both)
-        got = own * here[:, :, None] + got[:, :half].astype(f32) * there[:, :, None]
+        got = near[:, :, part] * here[:, :, None] + got[:, :half].astype(f32) * there[:, :, None]
         sums.append(got.astype(f16))
         sum_squares.append(both)
     packed = sums + [levels(jnp.concatenate(sum_squares, axis=1), width)]

time: 204 us -> 204 us (level)
  matrix products: 15.8 us -> 11.6 us
  other arithmetic: 14 us -> 17.1 us
    dot_general x4 -> x2, matrix products: 8.41 us -> 4.19 us  [partial(): jnp.dot(block, head, preferred_element_type=f32)]
    all_to_all x2, waiting for transfers between devices: 26.5 us -> 23 us  [exchange(): return lax.all_to_all(a, PLANE, 0, 0, axis_index_groups=SAME_CORE)]
    concatenate x1 -> x2, other arithmetic: 0.14 us -> 3.3 us  [the longest x1 3.16 us: body(): head = jnp.concatenate([head_weight, head_other], axis=1)]
  transfers between devices with their start and end apart: 10 -> 10, of which waited for: 4 -> 5; matrix products, arithmetic and copies ran while one was open for 7% -> 7% of each run, Pallas kernels for 0% -> 0%
where the time goes in v3:
time: 204 us; the launch traced here: 203 us
  waiting for transfers between devices  58.4 us (29%)
  starting transfers between devices  56.1 us (28%)
  blocking collectives  50.9 us (25%)
  other arithmetic  17.1 us (8%)
  matrix products  11.6 us (6%)
  local copies, waits for them, and re-layouts  7.37 us (4%)
    all_gather x1, blocking collectives, body(): every = lax.all_gather(sent, 'dp', axis=1)  50.9 us
    all_to_all x1, waiting for transfers between devices, body(): got = lax.all_to_all(packed, 'dp', 0, 0, axis_index_groups=SAME_PARITY)  28.7 us
    all_to_all x2, waiting for transfers between devices, exchange(): return lax.all_to_all(a, PLANE, 0, 0, axis_index_groups=SAME_CORE)  23 us
    ppermute x4, starting transfers between devices, swap_cores(): return lax.ppermute(a, 'tensor', CORE_PAIRS)  18.6 us
    all_to_all x1, starting transfers between devices, body(): lax.all_to_all(jnp.broadcast_to(own, (2 * PEERS,) + own.shape), PLANE, 0, 0)  11.4 us
    all_to_all x2, starting transfers between devices, exchange(): return lax.all_to_all(a, PLANE, 0, 0, axis_index_groups=SAME_CORE)  11.3 us
    all_to_all x1, starting transfers between devices, body(): got = lax.all_to_all(packed, 'dp', 0, 0, axis_index_groups=SAME_PARITY)  9.38 us
    dot_general x2, matrix products, joined_part(): jnp.dot(block, fc_weight, preferred_element_type=f32) * (PARTIAL / UP)  7.38 us
  transfers between devices with their start and end apart: 10, of which 5 were waited for; matrix products, arithmetic and copies ran while one was open for 7% of the time, Pallas kernels for 0%

profile of v3, /device:TPU:65, one launch (start us, length us, event | category | flops | bytes accessed | tf_op | source)
XLA Modules:
  0.0 202.5 jit_solution(4854362806449613168)
XLA Ops:
  0.7 1.1 multiply_convert_fusion.1
  1.8 50.9 %all-gather.1 = f16[2,16,32,1536]{3,2,1,0:T(8,128)(2,1)} all-gather(f16[2,1,32,1536]{3,2,1,0:T(8,128)(2,1)S(1)} %bitcast.81), channel_id=1, replica_groups=mesh['dp'=16,'tensor'=8,'vocab'=4] {'dp'}, dimensions={1}, use_global_device_ids=true | all-gather | bytes 3342336 | tf_op jit(solution)/shard_map/all_gather | solution.py:63
  52.7 4.2 %multiply_convert_fusion = f16[16,32,1024]{2,1,0:T(8,128)(2,1)} fusion(bf16[1536,1024]{1,0:T(8,128)(2,1)S(1)} %copy-done, f16[2,16,32,1536]{3,2,1,0:T(8,128)(2,1)} %all-gather.1, s32[]{:T(128)S(6)} %select_n.50), kind=kOutput, calls=%fused_computation.12 | convolution fusion | flops 1612447744 | bytes 5767172 | tf_op jit(solution)/shard_map/dot_general | solution.py:67
  56.9 10.6 %collective-permute-start = (f16[16,32,1024]{2,1,0:T(8,128)(2,1)}, f16[16,32,1024]{2,1,0:T(8,128)(2,1)}, u32[]{:S(2)}, u32[]{:S(2)}) collective-permute-start(f16[16,32,1024]{2,1,0:T(8,128)(2,1)} %multiply_convert_fusion), channel_id=1, source_target_pairs={{0,4},{4,0},{8,12},{12,8},{16,20},{20,16},{24,28},{28,24},{1,5},{5... | collective-permute-start | bytes 3145736 | tf_op jit(solution)/shard_map/ppermute | solution.py:23
  67.5 3.2 %fusion.8 = f32[16,32,1024]{2,1,0:T(8,128)S(1)} fusion(bf16[1536,1024]{1,0:T(8,128)(2,1)S(1)} %copy-done, f16[2,16,32,1536]{3,2,1,0:T(8,128)(2,1)} %all-gather.1, s32[]{:T(128)S(6)} %select_n.49), kind=kOutput, calls=%fused_computation.13 | convolution fusion | flops 1611923456 | bytes 6815748 | tf_op jit(solution)/shard_map/dot_general | solution.py:67
  70.8 2.6 %add_convert_fusion = f16[16,32,1024]{2,1,0:T(8,128)(2,1)} fusion(f32[16,32,1024]{2,1,0:T(8,128)S(1)} %fusion.8, f16[16,32,1024]{2,1,0:T(8,128)(2,1)} %collective-permute-done), kind=kLoop, calls=%fused_computation.11 | loop fusion | flops 1572864 | bytes 4194304 | tf_op jit(solution)/shard_map/convert_element_type | solution.py:71
  73.4 6.9 %all-to-all-start = ((f16[16,32,1024]{2,1,0:T(8,128)(2,1)}), f16[16,32,1024]{2,1,0:T(8,128)(2,1)}, u32[]{:S(2)}, u32[]{:S(2)}) async-start(f16[16,32,1024]{2,1,0:T(8,128)(2,1)} %add_convert_fusion), calls=%async_computation | async-start | bytes 2097152 | tf_op jit(solution)/shard_map/all_to_all | solution.py:33
  80.3 2.2 %collective-permute-start.2 = (bf16[1024,512]{1,0:T(8,128)(2,1)}, bf16[1024,512]{1,0:T(8,128)(2,1)}, u32[]{:S(2)}, u32[]{:S(2)}) collective-permute-start(bf16[1024,512]{1,0:T(8,128)(2,1)} %param.10), channel_id=1, source_target_pairs={{0,4},{4,0},{8,12},{12,8},{16,20},{20,16},{24,28},{28,24},{1,5},{5... | collective-permute-start | bytes 3145736 | tf_op jit(solution)/shard_map/ppermute | solution.py:23
  82.6 14.8 %all-to-all-done = f16[16,32,1024]{2,1,0:T(8,128)(2,1)} async-done(((f16[16,32,1024]{2,1,0:T(8,128)(2,1)}), f16[16,32,1024]{2,1,0:T(8,128)(2,1)}, u32[]{:S(2)}, u32[]{:S(2)}) %all-to-all-start) | async-done | bytes 1048608 | tf_op jit(solution)/shard_map/all_to_all | solution.py:33
  97.4 1.4 convert_reduce_fusion
  98.8 1.1 broadcast_in_dim.7
  99.9 4.3 %all-to-all-start.1 = ((bf16[16,32,1024]{2,1,0:T(8,128)(2,1)}), bf16[16,32,1024]{2,1,0:T(8,128)(2,1)}, u32[]{:S(2)}, u32[]{:S(2)}) async-start(bf16[16,32,1024]{2,1,0:T(8,128)(2,1)} %broadcast_in_dim.7), calls=%async_computation.1 | async-start | bytes 2097152 | tf_op jit(solution)/shard_map/all_to_all | solution.py:33
  104.3 3.7 %collective-permute-start.1 = (s32[512]{0:T(512)S(1)}, s32[512]{0:T(512)S(1)}, u32[]{:S(2)}, u32[]{:S(2)}) collective-permute-start(s32[512]{0:T(512)S(1)} %copy-done.4), channel_id=1, source_target_pairs={{0,4},{4,0},{8,12},{12,8},{16,20},{20,16},{24,28},{28,24},{1,5},{5... | collective-permute-start | bytes 6152 | tf_op jit(solution)/shard_map/ppermute | solution.py:23
  108.0 3.2 %pad_maximum_fusion = bf16[1024,1024]{1,0:T(8,128)(2,1)} fusion(bf16[1024,512]{1,0:T(8,128)(2,1)} %collective-permute-done.2, bf16[1024,512]{1,0:T(8,128)(2,1)} %param.10), kind=kLoop, calls=%fused_computation.4 | loop fusion | flops 4194304 | bytes 4194304 | tf_op jit(solution)/shard_map/concatenate | solution.py:78
  111.2 8.2 %all-to-all-done.1 = bf16[16,32,1024]{2,1,0:T(8,128)(2,1)} async-done(((bf16[16,32,1024]{2,1,0:T(8,128)(2,1)}), bf16[16,32,1024]{2,1,0:T(8,128)(2,1)}, u32[]{:S(2)}, u32[]{:S(2)}) %all-to-all-start.1) | async-done | bytes 1048608 | tf_op jit(solution)/shard_map/all_to_all | solution.py:33
  119.4 1.6 multiply_reduce_fusion
  121.1 1.1 dynamic-slice_bitcast_fusion
  122.2 2.4 %fusion.22 = f16[8,32,1024]{2,0,1:T(8,128)(2,1)S(1)} fusion(bf16[1024,1024]{1,0:T(8,128)(2,1)} %pad_maximum_fusion, bf16[8,32,1024]{2,1,0:T(8,128)(2,1)S(1)} %dynamic-slice_bitcast_fusion, f32[8,32]{0,1:T(8,128)S(1)} %copy.99), kind=kOutput, calls=%fused_computation.21 | convolution fusion | flops 537395200 | bytes 3146752 | tf_op jit(solution)/shard_map/dot_general | solution.py:86
  124.9 2.1 %collective-permute-start.3 = (f16[8,40,512]{2,0,1:T(8,128)(2,1)S(1)}, f16[8,40,512]{2,0,1:T(8,128)(2,1)S(1)}, u32[]{:S(2)}, u32[]{:S(2)}) collective-permute-start(f16[8,40,512]{2,0,1:T(8,128)(2,1)S(1)} %get-tuple-element.24), channel_id=1, source_target_pairs={{0,32},{32,64},{64,96},{96,128},{128,160},{160,192},{192,224},{224... | collective-permute-start | bytes 983048 | tf_op jit(solution)/shard_map/ppermute | solution.py:96
  127.0 3.4 %collective-permute-start.4 = (f16[8,40,512]{2,0,1:T(8,128)(2,1)S(1)}, f16[8,40,512]{2,0,1:T(8,128)(2,1)S(1)}, u32[]{:S(2)}, u32[]{:S(2)}) collective-permute-start(f16[8,40,512]{2,0,1:T(8,128)(2,1)S(1)} %get-tuple-element.25), channel_id=1, source_target_pairs={{0,480},{32,0},{64,32},{96,64},{128,96},{160,128},{192,160},{224,1... | collective-permute-start | bytes 983048 | tf_op jit(solution)/shard_map/ppermute | solution.py:96
  130.3 1.8 fusion.6
  132.1 1.1 fusion.65
  133.2 1.9 collective-permute-done.4
  136.9 1.9 fusion.26
  139.1 1.0 copy.106
  140.1 9.4 %all-to-all-start.2 = ((f16[8,72,512]{2,1,0:T(8,128)(2,1)}), f16[8,72,512]{2,1,0:T(8,128)(2,1)}, u32[]{:S(2)}, u32[]{:S(2)}) async-start(f16[8,72,512]{2,1,0:T(8,128)(2,1)} %copy.106), calls=%async_computation.2 | async-start | bytes 1179648 | tf_op jit(solution)/shard_map/all_to_all | solution.py:105
  149.6 28.7 %all-to-all-done.2 = f16[8,72,512]{2,1,0:T(8,128)(2,1)} async-done(((f16[8,72,512]{2,1,0:T(8,128)(2,1)}), f16[8,72,512]{2,1,0:T(8,128)(2,1)}, u32[]{:S(2)}, u32[]{:S(2)}) %all-to-all-start.2) | async-done | bytes 589856 | tf_op jit(solution)/shard_map/all_to_all | solution.py:105
  178.3 0.8 fusion.64
  179.2 1.3 multiply_reduce_fusion.1
  181.9 11.4 %all-to-all-start.3 = ((f32[32,8,128]{2,1,0:T(8,128)}), f32[32,8,128]{2,1,0:T(8,128)S(1)}, u32[]{:S(2)}, u32[]{:S(2)}) async-start(f32[32,8,128]{2,1,0:T(8,128)} %broadcast_in_dim.9), calls=%async_computation.3 | async-start | bytes 262144 | tf_op jit(solution)/shard_map/all_to_all | solution.py:121
  194.0 2.1 %collective-permute-start.5 = (f32[32,512]{1,0:T(8,128)}, f32[32,512]{1,0:T(8,128)S(1)}, u32[]{:S(2)}, u32[]{:S(2)}) collective-permute-start(f32[32,512]{1,0:T(8,128)} %get-tuple-element.23), channel_id=1, source_target_pairs={{0,4},{4,0},{8,12},{12,8},{16,20},{20,16},{24,28},{28,24},{1,5},{5... | collective-permute-start | bytes 196616 | tf_op jit(solution)/shard_map/ppermute | solution.py:23
  196.2 4.8 %all-to-all-done.3 = f32[32,8,128]{2,1,0:T(8,128)S(1)} async-done(((f32[32,8,128]{2,1,0:T(8,128)}), f32[32,8,128]{2,1,0:T(8,128)S(1)}, u32[]{:S(2)}, u32[]{:S(2)}) %all-to-all-start.3) | async-done | bytes 131104 | tf_op jit(solution)/shard_map/all_to_all | solution.py:121
  (63 shorter events, 6.2 us)
Async XLA Ops:
  0.6 52.1 %copy-start = (bf16[1536,1024]{1,0:T(8,128)(2,1)S(1)}, bf16[1536,1024]{1,0:T(8,128)(2,1)}, u32[]{:S(2)}) copy-start(bf16[1536,1024]{1,0:T(8,128)(2,1)} %param.8) | copy-start | bytes 9437188
  56.9 13.9 %collective-permute-start = (f16[16,32,1024]{2,1,0:T(8,128)(2,1)}, f16[16,32,1024]{2,1,0:T(8,128)(2,1)}, u32[]{:S(2)}, u32[]{:S(2)}) collective-permute-start(f16[16,32,1024]{2,1,0:T(8,128)(2,1)} %multiply_convert_fusion), channel_id=1, source_target_pairs={{0,4},{4,0},{8,12},{12,8},{16,20},{20,16},{24,28},{28,24},{1,5},{5... | collective-permute-start | bytes 3145736 | tf_op jit(solution)/shard_map/ppermute | solution.py:23
  73.4 9.2 %copy-start.3 = (f32[1024]{0:T(1024)S(1)}, f32[1024]{0:T(1024)}, u32[]{:S(2)}) copy-start(f32[1024]{0:T(1024)} %param.9) | copy-start | bytes 12292
  73.4 24.0 %all-to-all-start = ((f16[16,32,1024]{2,1,0:T(8,128)(2,1)}), f16[16,32,1024]{2,1,0:T(8,128)(2,1)}, u32[]{:S(2)}, u32[]{:S(2)}) async-start(f16[16,32,1024]{2,1,0:T(8,128)(2,1)} %add_convert_fusion), calls=%async_computation | async-start | bytes 2097152 | tf_op jit(solution)/shard_map/all_to_all | solution.py:33
  80.3 27.7 %collective-permute-start.2 = (bf16[1024,512]{1,0:T(8,128)(2,1)}, bf16[1024,512]{1,0:T(8,128)(2,1)}, u32[]{:S(2)}, u32[]{:S(2)}) collective-permute-start(bf16[1024,512]{1,0:T(8,128)(2,1)} %param.10), channel_id=1, source_target_pairs={{0,4},{4,0},{8,12},{12,8},{16,20},{20,16},{24,28},{28,24},{1,5},{5... | collective-permute-start | bytes 3145736 | tf_op jit(solution)/shard_map/ppermute | solution.py:23
  82.6 21.7 %copy-start.4 = (s32[512]{0:T(512)S(1)}, s32[512]{0:T(512)}, u32[]{:S(2)}) copy-start(s32[512]{0:T(512)} %param.11) | copy-start | bytes 6148
  99.9 19.5 %all-to-all-start.1 = ((bf16[16,32,1024]{2,1,0:T(8,128)(2,1)}), bf16[16,32,1024]{2,1,0:T(8,128)(2,1)}, u32[]{:S(2)}, u32[]{:S(2)}) async-start(bf16[16,32,1024]{2,1,0:T(8,128)(2,1)} %broadcast_in_dim.7), calls=%async_computation.1 | async-start | bytes 2097152 | tf_op jit(solution)/shard_map/all_to_all | solution.py:33
  104.3 6.9 %collective-permute-start.1 = (s32[512]{0:T(512)S(1)}, s32[512]{0:T(512)S(1)}, u32[]{:S(2)}, u32[]{:S(2)}) collective-permute-start(s32[512]{0:T(512)S(1)} %copy-done.4), channel_id=1, source_target_pairs={{0,4},{4,0},{8,12},{12,8},{16,20},{20,16},{24,28},{28,24},{1,5},{5... | collective-permute-start | bytes 6152 | tf_op jit(solution)/shard_map/ppermute | solution.py:23
  124.6 5.7 %copy-start.1 = (bf16[1024,1024]{1,0:T(8,128)(2,1)S(1)}, bf16[1024,1024]{1,0:T(8,128)(2,1)}, u32[]{:S(2)}) copy-start(bf16[1024,1024]{1,0:T(8,128)(2,1)} %pad_maximum_fusion) | copy-start | bytes 6291460
  124.9 8.3 %collective-permute-start.3 = (f16[8,40,512]{2,0,1:T(8,128)(2,1)S(1)}, f16[8,40,512]{2,0,1:T(8,128)(2,1)S(1)}, u32[]{:S(2)}, u32[]{:S(2)}) collective-permute-start(f16[8,40,512]{2,0,1:T(8,128)(2,1)S(1)} %get-tuple-element.24), channel_id=1, source_target_pairs={{0,32},{32,64},{64,96},{96,128},{128,160},{160,192},{192,224},{224... | collective-permute-start | bytes 983048 | tf_op jit(solution)/shard_map/ppermute | solution.py:96
  127.0 8.1 %collective-permute-start.4 = (f16[8,40,512]{2,0,1:T(8,128)(2,1)S(1)}, f16[8,40,512]{2,0,1:T(8,128)(2,1)S(1)}, u32[]{:S(2)}, u32[]{:S(2)}) collective-permute-start(f16[8,40,512]{2,0,1:T(8,128)(2,1)S(1)} %get-tuple-element.25), channel_id=1, source_target_pairs={{0,480},{32,0},{64,32},{96,64},{128,96},{160,128},{192,160},{224,1... | collective-permute-start | bytes 983048 | tf_op jit(solution)/shard_map/ppermute | solution.py:96
  135.1 0.7 copy-start.2
  138.9 10.6 %copy-start.5 = (s32[64]{0:T(128)S(1)}, s32[64]{0:T(128)}, u32[]{:S(2)}) copy-start(s32[64]{0:T(128)} %param.12) | copy-start | bytes 772
  140.1 38.2 %all-to-all-start.2 = ((f16[8,72,512]{2,1,0:T(8,128)(2,1)}), f16[8,72,512]{2,1,0:T(8,128)(2,1)}, u32[]{:S(2)}, u32[]{:S(2)}) async-start(f16[8,72,512]{2,1,0:T(8,128)(2,1)} %copy.106), calls=%async_computation.2 | async-start | bytes 1179648 | tf_op jit(solution)/shard_map/all_to_all | solution.py:105
  181.9 19.0 %all-to-all-start.3 = ((f32[32,8,128]{2,1,0:T(8,128)}), f32[32,8,128]{2,1,0:T(8,128)S(1)}, u32[]{:S(2)}, u32[]{:S(2)}) async-start(f32[32,8,128]{2,1,0:T(8,128)} %broadcast_in_dim.9), calls=%async_computation.3 | async-start | bytes 262144 | tf_op jit(solution)/shard_map/all_to_all | solution.py:121
  194.0 7.8 %collective-permute-start.5 = (f32[32,512]{1,0:T(8,128)}, f32[32,512]{1,0:T(8,128)S(1)}, u32[]{:S(2)}, u32[]{:S(2)}) collective-permute-start(f32[32,512]{1,0:T(8,128)} %get-tuple-element.23), channel_id=1, source_target_pairs={{0,4},{4,0},{8,12},{12,8},{16,20},{20,16},{24,28},{28,24},{1,5},{5... | collective-permute-start | bytes 196616 | tf_op jit(solution)/shard_map/ppermute | solution.py:23

commit v4 on v3

--- a/solution.py
+++ b/solution.py
@@ -77,18 +77,18 @@
 
     head = jnp.concatenate([head_weight, head_other], axis=1)
     gain, _, head = lax.optimization_barrier((norm_gain, map_other, head))
-    own = scaled.astype(f32) * (1.0 / gain)
-    square = (jnp.mean(own * own, axis=2) + eps).reshape(Z // 2, 2, half)
     scaled = scaled.reshape(Z // 2, 2, half, depth)
 
-    def partial(h):
-        block = pick(scaled, h).reshape(-1, depth)
-        return jnp.dot(block, head, preferred_element_type=f32).reshape(-1, half, 2 * width)
+    def side(h):
+        block = pick(scaled, h)
+        own = block.astype(f32) * (1.0 / gain)
+        values = jnp.dot(block.reshape(-1, depth), head, preferred_element_type=f32)
+        return jnp.mean(own * own, axis=2) + eps, values.reshape(-1, half, 2 * width)
 
-    far_square, near_square = pick(square, 1 - parity), pick(square, parity)
-    far = (partial(1 - parity) * lax.rsqrt(far_square)[:, :, None]).astype(f16)
+    far_square, far = side(1 - parity)
+    far = (far * lax.rsqrt(far_square)[:, :, None]).astype(f16)
     far_level = levels(far_square, width)
-    near = lax.optimization_barrier(partial(parity))
+    near_square, near = lax.optimization_barrier(side(lax.optimization_barrier((parity, far))[0]))
     sums, sum_squares = [], []
     for v, by in ((0, 1), (1, -1)):
         part = slice(v * width, (v + 1) * width)

time: 204 us -> 205 us (level)
  waiting for transfers between devices: 58.4 us -> 52.9 us
  starting transfers between devices: 56.1 us -> 59.3 us
  other arithmetic: 17.1 us -> 20.1 us
    all_to_all x1, starting transfers between devices: 11.4 us -> 15.2 us  [body(): lax.all_to_all(jnp.broadcast_to(own, (2 * PEERS,) + own.shape), PLANE, 0, 0)]
    all_to_all x1, waiting for transfers between devices: 28.7 us -> 25.1 us  [body(): got = lax.all_to_all(packed, 'dp', 0, 0, axis_index_groups=SAME_PARITY)]
  transfers between devices with their start and end apart: 10 -> 10, of which waited for: 5 -> 4; matrix products, arithmetic and copies ran while one was open for 7% -> 8% of each run, Pallas kernels for 0% -> 0%
where the time goes in v4:
time: 205 us; the launch traced here: 203 us
  starting transfers between devices  59.3 us (29%)
  waiting for transfers between devices  52.9 us (26%)
  blocking collectives  50.9 us (25%)
  other arithmetic  20.1 us (10%)
  matrix products  12.5 us (6%)
  local copies, waits for them, and re-layouts  6.75 us (3%)
    all_gather x1, blocking collectives, body(): every = lax.all_gather(sent, 'dp', axis=1)  50.9 us
    all_to_all x1, waiting for transfers between devices, body(): got = lax.all_to_all(packed, 'dp', 0, 0, axis_index_groups=SAME_PARITY)  25.1 us
    all_to_all x2, waiting for transfers between devices, exchange(): return lax.all_to_all(a, PLANE, 0, 0, axis_index_groups=SAME_CORE)  23 us
    ppermute x4, starting transfers between devices, swap_cores(): return lax.ppermute(a, 'tensor', CORE_PAIRS)  18.6 us
    all_to_all x1, starting transfers between devices, body(): lax.all_to_all(jnp.broadcast_to(own, (2 * PEERS,) + own.shape), PLANE, 0, 0)  15.2 us
    all_to_all x2, starting transfers between devices, exchange(): return lax.all_to_all(a, PLANE, 0, 0, axis_index_groups=SAME_CORE)  11.3 us
    all_to_all x1, starting transfers between devices, body(): got = lax.all_to_all(packed, 'dp', 0, 0, axis_index_groups=SAME_PARITY)  8.96 us
    dot_general x2, matrix products, joined_part(): jnp.dot(block, fc_weight, preferred_element_type=f32) * (PARTIAL / UP)  7.38 us
  transfers between devices with their start and end apart: 10, of which 4 were waited for; matrix products, arithmetic and copies ran while one was open for 8% of the time, Pallas kernels for 0%

profile of v4, /device:TPU:65, one launch (start us, length us, event | category | flops | bytes accessed | tf_op | source)
XLA Modules:
  0.0 203.4 jit_solution(12332687578189864979)
XLA Ops:
  0.7 1.1 multiply_convert_fusion.1
  1.8 50.9 %all-gather.1 = f16[2,16,32,1536]{3,2,1,0:T(8,128)(2,1)} all-gather(f16[2,1,32,1536]{3,2,1,0:T(8,128)(2,1)S(1)} %bitcast.93), channel_id=1, replica_groups=mesh['dp'=16,'tensor'=8,'vocab'=4] {'dp'}, dimensions={1}, use_global_device_ids=true | all-gather | bytes 3342336 | tf_op jit(solution)/shard_map/all_gather | solution.py:63
  52.7 4.2 %multiply_convert_fusion = f16[16,32,1024]{2,1,0:T(8,128)(2,1)} fusion(bf16[1536,1024]{1,0:T(8,128)(2,1)S(1)} %copy-done, f16[2,16,32,1536]{3,2,1,0:T(8,128)(2,1)} %all-gather.1, s32[]{:T(128)S(6)} %select_n.47), kind=kOutput, calls=%fused_computation.11 | convolution fusion | flops 1612447744 | bytes 5767172 | tf_op jit(solution)/shard_map/dot_general | solution.py:67
  56.9 10.6 %collective-permute-start = (f16[16,32,1024]{2,1,0:T(8,128)(2,1)}, f16[16,32,1024]{2,1,0:T(8,128)(2,1)}, u32[]{:S(2)}, u32[]{:S(2)}) collective-permute-start(f16[16,32,1024]{2,1,0:T(8,128)(2,1)} %multiply_convert_fusion), channel_id=1, source_target_pairs={{0,4},{4,0},{8,12},{12,8},{16,20},{20,16},{24,28},{28,24},{1,5},{5... | collective-permute-start | bytes 3145736 | tf_op jit(solution)/shard_map/ppermute | solution.py:23
  67.5 3.2 %fusion.8 = f32[16,32,1024]{2,1,0:T(8,128)S(1)} fusion(bf16[1536,1024]{1,0:T(8,128)(2,1)S(1)} %copy-done, f16[2,16,32,1536]{3,2,1,0:T(8,128)(2,1)} %all-gather.1, s32[]{:T(128)S(6)} %select_n.46), kind=kOutput, calls=%fused_computation.12 | convolution fusion | flops 1611923456 | bytes 6815748 | tf_op jit(solution)/shard_map/dot_general | solution.py:67
  70.8 2.6 %add_convert_fusion = f16[16,32,1024]{2,1,0:T(8,128)(2,1)} fusion(f32[16,32,1024]{2,1,0:T(8,128)S(1)} %fusion.8, f16[16,32,1024]{2,1,0:T(8,128)(2,1)} %collective-permute-done), kind=kLoop, calls=%fused_computation.10 | loop fusion | flops 1572864 | bytes 4194304 | tf_op jit(solution)/shard_map/convert_element_type | solution.py:71
  73.4 6.9 %all-to-all-start = ((f16[16,32,1024]{2,1,0:T(8,128)(2,1)}), f16[16,32,1024]{2,1,0:T(8,128)(2,1)}, u32[]{:S(2)}, u32[]{:S(2)}) async-start(f16[16,32,1024]{2,1,0:T(8,128)(2,1)} %add_convert_fusion), calls=%async_computation | async-start | bytes 2097152 | tf_op jit(solution)/shard_map/all_to_all | solution.py:33
  80.3 2.2 %collective-permute-start.2 = (bf16[1024,512]{1,0:T(8,128)(2,1)}, bf16[1024,512]{1,0:T(8,128)(2,1)}, u32[]{:S(2)}, u32[]{:S(2)}) collective-permute-start(bf16[1024,512]{1,0:T(8,128)(2,1)} %param.10), channel_id=1, source_target_pairs={{0,4},{4,0},{8,12},{12,8},{16,20},{20,16},{24,28},{28,24},{1,5},{5... | collective-permute-start | bytes 3145736 | tf_op jit(solution)/shard_map/ppermute | solution.py:23
  82.6 14.8 %all-to-all-done = f16[16,32,1024]{2,1,0:T(8,128)(2,1)} async-done(((f16[16,32,1024]{2,1,0:T(8,128)(2,1)}), f16[16,32,1024]{2,1,0:T(8,128)(2,1)}, u32[]{:S(2)}, u32[]{:S(2)}) %all-to-all-start) | async-done | bytes 1048608 | tf_op jit(solution)/shard_map/all_to_all | solution.py:33
  97.4 1.4 convert_reduce_fusion
  98.8 1.1 broadcast_in_dim.7
  99.9 4.3 %all-to-all-start.1 = ((bf16[16,32,1024]{2,1,0:T(8,128)(2,1)}), bf16[16,32,1024]{2,1,0:T(8,128)(2,1)}, u32[]{:S(2)}, u32[]{:S(2)}) async-start(bf16[16,32,1024]{2,1,0:T(8,128)(2,1)} %broadcast_in_dim.7), calls=%async_computation.1 | async-start | bytes 2097152 | tf_op jit(solution)/shard_map/all_to_all | solution.py:33
  104.3 3.7 %collective-permute-start.1 = (s32[512]{0:T(512)S(1)}, s32[512]{0:T(512)S(1)}, u32[]{:S(2)}, u32[]{:S(2)}) collective-permute-start(s32[512]{0:T(512)S(1)} %copy-done.2), channel_id=1, source_target_pairs={{0,4},{4,0},{8,12},{12,8},{16,20},{20,16},{24,28},{28,24},{1,5},{5... | collective-permute-start | bytes 6152 | tf_op jit(solution)/shard_map/ppermute | solution.py:23
  108.0 3.2 %pad_maximum_fusion = bf16[1024,1024]{1,0:T(8,128)(2,1)} fusion(bf16[1024,512]{1,0:T(8,128)(2,1)} %collective-permute-done.2, bf16[1024,512]{1,0:T(8,128)(2,1)} %param.10), kind=kLoop, calls=%fused_computation.4 | loop fusion | flops 4194304 | bytes 4194304 | tf_op jit(solution)/shard_map/concatenate | solution.py:78
  111.2 8.2 %all-to-all-done.1 = bf16[16,32,1024]{2,1,0:T(8,128)(2,1)} async-done(((bf16[16,32,1024]{2,1,0:T(8,128)(2,1)}), bf16[16,32,1024]{2,1,0:T(8,128)(2,1)}, u32[]{:S(2)}, u32[]{:S(2)}) %all-to-all-start.1) | async-done | bytes 1048608 | tf_op jit(solution)/shard_map/all_to_all | solution.py:33
  119.4 2.0 multiply_reduce_fusion.2
  121.5 2.6 %fusion.22 = f16[8,32,1024]{2,0,1:T(8,128)(2,1)S(1)} fusion(bf16[1024,1024]{1,0:T(8,128)(2,1)} %pad_maximum_fusion, bf16[8,32,1024]{2,1,0:T(8,128)(2,1)} %get-tuple-element.21, f32[8,32]{0,1:T(8,128)S(1)} %copy.71), kind=kOutput, calls=%fused_computation.20 | convolution fusion | flops 537395200 | bytes 3146752 | tf_op jit(solution)/shard_map/dot_general | solution.py:85
  124.9 1.9 pad_maximum_fusion.3
  126.8 1.9 collective-permute-start.3
  128.7 3.4 %collective-permute-start.4 = (f16[8,40,512]{2,0,1:T(8,128)(2,1)}, f16[8,40,512]{2,0,1:T(8,128)(2,1)}, u32[]{:S(2)}, u32[]{:S(2)}) collective-permute-start(f16[8,40,512]{2,0,1:T(8,128)(2,1)} %get-tuple-element.35), channel_id=1, source_target_pairs={{0,480},{32,0},{64,32},{96,64},{128,96},{160,128},{192,160},{224,1... | collective-permute-start | bytes 983048 | tf_op jit(solution)/shard_map/ppermute | solution.py:96
  132.1 1.3 multiply_reduce_fusion.1
  133.4 2.5 %fusion.4 = f32[8,32,1024]{2,1,0:T(8,128)S(1)} fusion(bf16[1024,1024]{1,0:T(8,128)(2,1)} %pad_maximum_fusion, bf16[8,2,32,1024]{3,2,1,0:T(8,128)(2,1)} %bitcast.4, s32[]{:T(128)S(6)} %select_n.50), kind=kOutput, calls=%fused_computation.5 | convolution fusion | flops 536870912 | bytes 3670020 | tf_op jit(solution)/shard_map/dot_general | solution.py:85
  135.9 1.6 copy.73
  138.6 1.5 fusion.28
  140.3 1.0 copy.79
  141.3 9.0 %all-to-all-start.2 = ((f16[8,72,512]{2,1,0:T(8,128)(2,1)}), f16[8,72,512]{2,1,0:T(8,128)(2,1)}, u32[]{:S(2)}, u32[]{:S(2)}) async-start(f16[8,72,512]{2,1,0:T(8,128)(2,1)} %copy.79), calls=%async_computation.2 | async-start | bytes 1179648 | tf_op jit(solution)/shard_map/all_to_all | solution.py:105
  150.4 25.1 %all-to-all-done.2 = f16[8,72,512]{2,1,0:T(8,128)(2,1)} async-done(((f16[8,72,512]{2,1,0:T(8,128)(2,1)}), f16[8,72,512]{2,1,0:T(8,128)(2,1)}, u32[]{:S(2)}, u32[]{:S(2)}) %all-to-all-start.2) | async-done | bytes 589856 | tf_op jit(solution)/shard_map/all_to_all | solution.py:105
  175.5 0.8 fusion.66
  176.4 1.3 multiply_reduce_fusion
  179.1 15.2 %all-to-all-start.3 = ((f32[32,8,128]{2,1,0:T(8,128)}), f32[32,8,128]{2,1,0:T(8,128)S(1)}, u32[]{:S(2)}, u32[]{:S(2)}) async-start(f32[32,8,128]{2,1,0:T(8,128)} %broadcast_in_dim.9), calls=%async_computation.3 | async-start | bytes 262144 | tf_op jit(solution)/shard_map/all_to_all | solution.py:121
  194.9 2.1 %collective-permute-start.5 = (f32[32,512]{1,0:T(8,128)}, f32[32,512]{1,0:T(8,128)S(1)}, u32[]{:S(2)}, u32[]{:S(2)}) collective-permute-start(f32[32,512]{1,0:T(8,128)} %get-tuple-element.33), channel_id=1, source_target_pairs={{0,4},{4,0},{8,12},{12,8},{16,20},{20,16},{24,28},{28,24},{1,5},{5... | collective-permute-start | bytes 196616 | tf_op jit(solution)/shard_map/ppermute | solution.py:23
  197.1 4.8 %all-to-all-done.3 = f32[32,8,128]{2,1,0:T(8,128)S(1)} async-done(((f32[32,8,128]{2,1,0:T(8,128)}), f32[32,8,128]{2,1,0:T(8,128)S(1)}, u32[]{:S(2)}, u32[]{:S(2)}) %all-to-all-start.3) | async-done | bytes 131104 | tf_op jit(solution)/shard_map/all_to_all | solution.py:121
  (62 shorter events, 6.1 us)
Async XLA Ops:
  0.6 52.1 %copy-start = (bf16[1536,1024]{1,0:T(8,128)(2,1)S(1)}, bf16[1536,1024]{1,0:T(8,128)(2,1)}, u32[]{:S(2)}) copy-start(bf16[1536,1024]{1,0:T(8,128)(2,1)} %param.8) | copy-start | bytes 9437188
  56.9 13.9 %collective-permute-start = (f16[16,32,1024]{2,1,0:T(8,128)(2,1)}, f16[16,32,1024]{2,1,0:T(8,128)(2,1)}, u32[]{:S(2)}, u32[]{:S(2)}) collective-permute-start(f16[16,32,1024]{2,1,0:T(8,128)(2,1)} %multiply_convert_fusion), channel_id=1, source_target_pairs={{0,4},{4,0},{8,12},{12,8},{16,20},{20,16},{24,28},{28,24},{1,5},{5... | collective-permute-start | bytes 3145736 | tf_op jit(solution)/shard_map/ppermute | solution.py:23
  73.4 9.2 %copy-start.1 = (f32[1024]{0:T(1024)S(1)}, f32[1024]{0:T(1024)}, u32[]{:S(2)}) copy-start(f32[1024]{0:T(1024)} %param.9) | copy-start | bytes 12292
  73.4 24.0 %all-to-all-start = ((f16[16,32,1024]{2,1,0:T(8,128)(2,1)}), f16[16,32,1024]{2,1,0:T(8,128)(2,1)}, u32[]{:S(2)}, u32[]{:S(2)}) async-start(f16[16,32,1024]{2,1,0:T(8,128)(2,1)} %add_convert_fusion), calls=%async_computation | async-start | bytes 2097152 | tf_op jit(solution)/shard_map/all_to_all | solution.py:33
  80.3 27.7 %collective-permute-start.2 = (bf16[1024,512]{1,0:T(8,128)(2,1)}, bf16[1024,512]{1,0:T(8,128)(2,1)}, u32[]{:S(2)}, u32[]{:S(2)}) collective-permute-start(bf16[1024,512]{1,0:T(8,128)(2,1)} %param.10), channel_id=1, source_target_pairs={{0,4},{4,0},{8,12},{12,8},{16,20},{20,16},{24,28},{28,24},{1,5},{5... | collective-permute-start | bytes 3145736 | tf_op jit(solution)/shard_map/ppermute | solution.py:23
  82.6 21.7 %copy-start.2 = (s32[512]{0:T(512)S(1)}, s32[512]{0:T(512)}, u32[]{:S(2)}) copy-start(s32[512]{0:T(512)} %param.11) | copy-start | bytes 6148
  99.9 19.5 %all-to-all-start.1 = ((bf16[16,32,1024]{2,1,0:T(8,128)(2,1)}), bf16[16,32,1024]{2,1,0:T(8,128)(2,1)}, u32[]{:S(2)}, u32[]{:S(2)}) async-start(bf16[16,32,1024]{2,1,0:T(8,128)(2,1)} %broadcast_in_dim.7), calls=%async_computation.1 | async-start | bytes 2097152 | tf_op jit(solution)/shard_map/all_to_all | solution.py:33
  104.3 6.9 %collective-permute-start.1 = (s32[512]{0:T(512)S(1)}, s32[512]{0:T(512)S(1)}, u32[]{:S(2)}, u32[]{:S(2)}) collective-permute-start(s32[512]{0:T(512)S(1)} %copy-done.2), channel_id=1, source_target_pairs={{0,4},{4,0},{8,12},{12,8},{16,20},{20,16},{24,28},{28,24},{1,5},{5... | collective-permute-start | bytes 6152 | tf_op jit(solution)/shard_map/ppermute | solution.py:23
  111.2 10.2 %copy-start.3 = (s32[512]{0:T(512)}, s32[512]{0:T(512)S(1)}, u32[]{:S(2)}) copy-start(s32[512]{0:T(512)S(1)} %collective-permute-done.1) | copy-start | bytes 6148
  126.8 10.7 %collective-permute-start.3 = (f16[8,40,512]{2,0,1:T(8,128)(2,1)}, f16[8,40,512]{2,0,1:T(8,128)(2,1)S(1)}, u32[]{:S(2)}, u32[]{:S(2)}) collective-permute-start(f16[8,40,512]{2,0,1:T(8,128)(2,1)} %get-tuple-element.34), channel_id=1, source_target_pairs={{0,32},{32,64},{64,96},{96,128},{128,160},{160,192},{192,224},{224... | collective-permute-start | bytes 983048 | tf_op jit(solution)/shard_map/ppermute | solution.py:96
  128.7 8.7 %collective-permute-start.4 = (f16[8,40,512]{2,0,1:T(8,128)(2,1)}, f16[8,40,512]{2,0,1:T(8,128)(2,1)}, u32[]{:S(2)}, u32[]{:S(2)}) collective-permute-start(f16[8,40,512]{2,0,1:T(8,128)(2,1)} %get-tuple-element.35), channel_id=1, source_target_pairs={{0,480},{32,0},{64,32},{96,64},{128,96},{160,128},{192,160},{224,1... | collective-permute-start | bytes 983048 | tf_op jit(solution)/shard_map/ppermute | solution.py:96
  140.1 10.2 %copy-start.5 = (s32[64]{0:T(128)S(1)}, s32[64]{0:T(128)}, u32[]{:S(2)}) copy-start(s32[64]{0:T(128)} %param.12) | copy-start | bytes 772
  140.1 10.3 %copy-start.4 = (s32[512]{0:T(512)S(1)}, s32[512]{0:T(512)}, u32[]{:S(2)}) copy-start(s32[512]{0:T(512)} %copy-done.3) | copy-start | bytes 6148
  141.3 34.2 %all-to-all-start.2 = ((f16[8,72,512]{2,1,0:T(8,128)(2,1)}), f16[8,72,512]{2,1,0:T(8,128)(2,1)}, u32[]{:S(2)}, u32[]{:S(2)}) async-start(f16[8,72,512]{2,1,0:T(8,128)(2,1)} %copy.79), calls=%async_computation.2 | async-start | bytes 1179648 | tf_op jit(solution)/shard_map/all_to_all | solution.py:105
  179.1 22.8 %all-to-all-start.3 = ((f32[32,8,128]{2,1,0:T(8,128)}), f32[32,8,128]{2,1,0:T(8,128)S(1)}, u32[]{:S(2)}, u32[]{:S(2)}) async-start(f32[32,8,128]{2,1,0:T(8,128)} %broadcast_in_dim.9), calls=%async_computation.3 | async-start | bytes 262144 | tf_op jit(solution)/shard_map/all_to_all | solution.py:121
  194.9 7.8 %collective-permute-start.5 = (f32[32,512]{1,0:T(8,128)}, f32[32,512]{1,0:T(8,128)S(1)}, u32[]{:S(2)}, u32[]{:S(2)}) collective-permute-start(f32[32,512]{1,0:T(8,128)} %get-tuple-element.33), channel_id=1, source_target_pairs={{0,4},{4,0},{8,12},{12,8},{16,20},{20,16},{24,28},{28,24},{1,5},{5... | collective-permute-start | bytes 196616 | tf_op jit(solution)/shard_map/ppermute | solution.py:23
